TPU v7x, 128 devices: a whole 4x4x4 slice. The times are simulated.
128 devices in a mesh: seq: 16 (over x, y), tp: 8 (over z, core).
Axes of the slice: x: 4, y: 4, z: 4, core: 2. Of those that a mesh axis runs over, the one named last changes fastest.
Arguments:
- hidden: bfloat16 [2048, 5120], P(('seq', 'tp')), may hold values from -6 to 6
- query_weight: bfloat16 [5120, 8192], P(None, 'tp'), may hold values from -0.078125 to 0.078125
- key_weight: bfloat16 [5120, 1024], P(None, 'tp'), may hold values from -0.078125 to 0.078125
- value_weight: bfloat16 [5120, 1024], P(None, 'tp'), may hold values from -0.078125 to 0.078125
- prefix_cache: bfloat16 [32768, 8, 2, 128], P('seq', 'tp'), may hold values from -10.4 to 10.4
- owner_prompt: int32 [16], P('seq'), may hold values from 0 to 3, as said below
- response_length: int32 [64], P('seq'), may hold values from 1 to 32
- context_grad: bfloat16 [2048, 8192], P('seq', 'tp'), may hold values from -6 to 6
Outputs:
- context: bfloat16 [2048, 8192], P('seq', 'tp')
- hidden_grad: bfloat16 [2048, 5120], P(('seq', 'tp'))
- prefix_grad: bfloat16 [32768, 8, 2, 128], P('seq', 'tp')
Inputs may be any that keep to these rules, and one draw needn't show every extreme that they name: `owner_prompt`: each prompt index appears exactly 16 / 4 times.
All inputs are finite; a program needn't handle non-finite values.
Results may differ from a plain program's by a relative error of at most 0.024.
Values may be sent and summed in bfloat16 or wider, within the bound.
No kernel may reach another device: no remote copies, remote signals or barrier semaphores. Data moves between devices by JAX's collectives and lax.ppermute only.
A program may use at most 192 MiB of HBM per device.

v0:
```python
import jax
import jax.numpy as jnp
from jax import lax
from jax.sharding import PartitionSpec as P

QH = 64
KVH = 8
HD = 128
PREFIX = 8192
RESP_LEN = 32


big_negative = -1e30


def key_block():
    return 1024


def contract(grads, weight):
    return lax.dot_general(
        grads, weight, (((1,), (1,)), ((), ())), preferred_element_type=jnp.float32
    )


def forward_block(running, queries, block_keys, block_values, usable, score_scale):
    row_max, row_sum, weighted = running
    scores = (
        jnp.einsum("rgjd,kgd->gjrk", queries, block_keys, preferred_element_type=jnp.float32)
        * score_scale
    )
    scores = jnp.where(usable, scores, big_negative)
    new_max = jnp.maximum(row_max, jnp.max(scores, axis=-1))
    factor = jnp.exp(row_max - new_max)
    unnormed = jnp.where(usable, jnp.exp(scores - new_max[..., None]), 0.0)
    row_sum = row_sum * factor + jnp.sum(unnormed, axis=-1)
    portion = jnp.einsum(
        "gjrk,kgd->rgjd",
        unnormed.astype(jnp.bfloat16),
        block_values,
        preferred_element_type=jnp.float32,
    )
    weighted = weighted * jnp.transpose(factor, (2, 0, 1))[..., None] + portion
    return (new_max, row_sum, weighted)


def backward_block(
    query_grad,
    queries,
    out_grad,
    log_norm,
    correction,
    block_keys,
    block_values,
    usable,
    score_scale,
):
    scores = (
        jnp.einsum("rgjd,kgd->gjrk", queries, block_keys, preferred_element_type=jnp.float32)
        * score_scale
    )
    attention = jnp.where(usable, jnp.exp(scores - log_norm[..., None]), 0.0)
    weight_grad = jnp.einsum(
        "rgjd,kgd->gjrk", out_grad, block_values, preferred_element_type=jnp.float32
    )
    score_grad = attention * (weight_grad - correction[..., None])
    grad_round = score_grad.astype(jnp.bfloat16)
    query_grad = (
        query_grad
        + jnp.einsum("gjrk,kgd->rgjd", grad_round, block_keys, preferred_element_type=jnp.float32)
        * score_scale
    )
    key_part = (
        jnp.einsum("gjrk,rgjd->kgd", grad_round, queries, preferred_element_type=jnp.float32)
        * score_scale
    )
    value_part = jnp.einsum(
        "gjrk,rgjd->kgd",
        attention.astype(jnp.bfloat16),
        out_grad,
        preferred_element_type=jnp.float32,
    )
    return (query_grad, key_part, value_part)


def on_device(
    hidden,
    query_weight,
    key_weight,
    value_weight,
    prefix_cache,
    owner_prompt,
    response_length,
    context_grad,
):
    score_scale = HD ** (-0.5)
    query_group = QH // KVH
    local_heads = key_weight.shape[1] // HD
    query_cols = query_weight.shape[1]
    key_cols = key_weight.shape[1]
    segment = lax.all_gather(hidden, "tp", axis=0, tiled=True)
    projected = jnp.concatenate(
        [
            jnp.dot(segment, query_weight, preferred_element_type=jnp.float32).astype(jnp.bfloat16),
            jnp.dot(segment, key_weight, preferred_element_type=jnp.float32).astype(jnp.bfloat16),
            jnp.dot(segment, value_weight, preferred_element_type=jnp.float32).astype(jnp.bfloat16),
        ],
        axis=1,
    )
    row_count = projected.shape[0]
    queries = projected[:, :query_cols].reshape(row_count, local_heads, query_group, HD)
    key_rows = projected[:, query_cols : query_cols + key_cols].reshape(row_count, local_heads, HD)
    value_rows = projected[:, query_cols + key_cols :].reshape(row_count, local_heads, HD)
    own_prompt = owner_prompt[0]
    position = jnp.arange(row_count, dtype=jnp.int32) % RESP_LEN
    member = jnp.arange(row_count, dtype=jnp.int32) // RESP_LEN
    length_rows = jnp.repeat(response_length, RESP_LEN)
    live_rows = position < length_rows
    causal = (
        (member[:, None] == member[None, :])
        & (position[None, :] <= position[:, None])
        & live_rows[None, :]
    )
    causal_usable = causal[None, None, :, :]
    initial = (
        jnp.full((local_heads, query_group, row_count), big_negative, jnp.float32),
        jnp.zeros((local_heads, query_group, row_count), jnp.float32),
        jnp.zeros((row_count, local_heads, query_group, HD), jnp.float32),
    )
    running = initial
    gathered = lax.all_gather(prefix_cache, "seq", axis=0, tiled=True)
    own_prefix = lax.dynamic_slice_in_dim(gathered, own_prompt * PREFIX, PREFIX, 0)
    block_size = key_block()

    def forward_local(block_index, current):
        block_rows = lax.dynamic_slice_in_dim(own_prefix, block_index * block_size, block_size, 0)
        return forward_block(
            current, queries, block_rows[:, :, 0], block_rows[:, :, 1], True, score_scale
        )

    running = lax.fori_loop(0, PREFIX // block_size, forward_local, running)
    running = forward_block(running, queries, key_rows, value_rows, causal_usable, score_scale)
    row_max, row_sum, weighted = running
    log_norm = row_max + jnp.log(row_sum)
    context = weighted / jnp.transpose(row_sum, (2, 0, 1))[..., None]
    context = jnp.where(live_rows[:, None, None, None], context, 0.0).astype(jnp.bfloat16)
    out_grad = jnp.where(live_rows[:, None], context_grad, jnp.zeros_like(context_grad))
    out_grad = out_grad.reshape(row_count, local_heads, query_group, HD)
    correction = jnp.sum(out_grad.astype(jnp.float32) * context.astype(jnp.float32), axis=-1)
    correction = jnp.transpose(correction, (1, 2, 0))
    query_grad = jnp.zeros((row_count, local_heads, query_group, HD), jnp.float32)
    query_grad, key_grad, value_grad = backward_block(
        query_grad,
        queries,
        out_grad,
        log_norm,
        correction,
        key_rows,
        value_rows,
        causal_usable,
        score_scale,
    )
    seq_count = lax.axis_size("seq")
    prefix_total = jnp.zeros((prefix_cache.shape[0] * seq_count, local_heads, 2, HD), jnp.bfloat16)

    def backward_local(block_index, carried):
        grad_rows, grad_cache = carried
        block_rows = lax.dynamic_slice_in_dim(own_prefix, block_index * block_size, block_size, 0)
        grad_rows, key_part, value_part = backward_block(
            grad_rows,
            queries,
            out_grad,
            log_norm,
            correction,
            block_rows[:, :, 0],
            block_rows[:, :, 1],
            True,
            score_scale,
        )
        row_start = own_prompt * PREFIX + block_index * block_size
        written = jnp.stack([key_part, value_part], axis=2).astype(jnp.bfloat16)
        grad_cache = lax.dynamic_update_slice(grad_cache, written, (row_start, 0, 0, 0))
        return (grad_rows, grad_cache)

    query_grad, prefix_total = lax.fori_loop(
        0, PREFIX // block_size, backward_local, (query_grad, prefix_total)
    )
    prefix_grad = (
        lax.psum_scatter(prefix_total, "seq", scatter_dimension=0, tiled=True)
        .astype(jnp.float32)
        .astype(jnp.bfloat16)
    )
    query_grad = query_grad.astype(jnp.bfloat16).reshape(row_count, query_cols)
    key_grad = key_grad.astype(jnp.bfloat16).reshape(row_count, key_cols)
    value_grad = value_grad.astype(jnp.bfloat16).reshape(row_count, key_cols)
    hidden_grad = lax.psum_scatter(
        (
            contract(query_grad, query_weight)
            + contract(key_grad, key_weight)
            + contract(value_grad, value_weight)
        ).astype(jnp.bfloat16),
        "tp",
        scatter_dimension=0,
        tiled=True,
    )
    return (context.reshape(row_count, query_cols), hidden_grad, prefix_grad)


def solution(mesh):
    return jax.shard_map(
        on_device,
        mesh=mesh,
        in_specs=(
            P(("seq", "tp"), None),
            P(None, "tp"),
            P(None, "tp"),
            P(None, "tp"),
            P("seq", "tp", None, None),
            P("seq"),
            P("seq"),
            P("seq", "tp"),
        ),
        out_specs=(P("seq", "tp"), P(("seq", "tp"), None), P("seq", "tp", None, None)),
        check_vma=False,
    )
```

profile of v0, /device:TPU:0, one launch (start us, length us, event | category | flops | bytes accessed | tf_op | source)
XLA Modules:
  0.0 531.3 jit_solution(17930079630713252344)
XLA Ops:
  8.0 2.3 copy.36
  13.4 23.1 %all-gather.5.cloned.1.call-done = bf16[128,5120]{1,0:T(8,128)(2,1)} async-done(((bf16[16,5120]{1,0:T(8,128)(2,1)}), bf16[128,5120]{1,0:T(8,128)(2,1)}) %all-gather.5.cloned.1.call-update) | async-done | bytes 1310736 | tf_op jit(solution)/shard_map/all_gather | solution.py:101
  36.5 6.0 %convolution_convert_fusion = bf16[128,1024]{1,0:T(8,128)(2,1)S(1)} fusion(bf16[128,5120]{1,0:T(8,128)(2,1)} %all-gather.5.cloned.1.call-done, bf16[5120,1024]{1,0:T(8,128)(2,1)} %param.13), kind=kOutput, calls=%fused_computation.77 | convolution fusion | flops 1342308352 | bytes 12058624 | tf_op jit(solution)/shard_map/dot_general | solution.py:104
  44.3 106.1 %all-gather.3.cloned.1.call-done = bf16[32768,1,2,128]{3,0,2,1:T(8,128)(2,1)} async-done(((bf16[2048,1,2,128]{3,0,2,1:T(8,128)(2,1)}), bf16[32768,1,2,128]{3,0,2,1:T(8,128)(2,1)}) %all-gather.3.cloned.1.call-update) | async-done | bytes 16777232 | tf_op jit(solution)/shard_map/all_gather | solution.py:131
  150.4 4.4 constant_dynamic-slice_fusion.1
  154.8 35.4 %while.36 = (s32[]{:T(128)}, f32[1,8,128]{2,1,0:T(8,128)S(1)}, f32[1,8,128]{2,1,0:T(8,128)S(1)}, f32[128,1,8,128]{0,3,2,1:T(8,128)S(1)}, bf16[8192,1,2,128]{3,0,...) while((s32[]{:T(128)}, f32[1,8,128]{2,1,0:T(8,128)S(1)}, ...), condition=%wide.region_3.4_spmd.clone, body=%wide.region_0.3_spmd.clone.sunk | while | flops 545658880 | bytes 14483655 | solution.py:141
  157.2 2.0 fusion.168
  161.6 2.0 fusion.168
  193.6 10.1 %broadcast_in_dim.103.clone = bf16[32768,1,2,128]{3,2,1,0:T(2,128)(2,1)} broadcast(bf16[]{:T(256)} %constant.175.clone.1), dimensions={} | broadcast | bytes 16777218 | tf_op jit(solution)/shard_map/broadcast_in_dim | solution.py:164
  203.7 65.4 %while.35 = (s32[]{:T(128)}, f32[128,1,8,128]{0,3,2,1:T(8,128)S(1)}, bf16[32768,1,2,128]{3,2,1,0:T(2,128)(2,1)}, bf16[8192,1,2,128]{3,0,2,1:T(8,128)(2,1)}, bf16...) while((s32[]{:T(128)}, ...), condition=%wide.region_8.9_spmd, body=%wide.region_7.8_spmd.sunk | while | flops 1351483392 | bytes 24391944 | solution.py:185
  206.2 2.1 fusion.161
  214.3 2.1 fusion.161
  222.5 2.1 fusion.161
  230.7 2.1 fusion.161
  238.9 2.1 fusion.161
  247.0 2.1 fusion.161
  255.2 2.1 fusion.161
  263.4 2.1 fusion.161
  271.4 9.1 %fusion.112 = f32[128,5120]{1,0:T(8,128)} fusion(bf16[128,1024]{0,1:T(8,128)(2,1)S(1)} %bitcast.406, bf16[5120,1024]{1,0:T(8,128)(2,1)} %param.13), kind=kOutput, calls=%fused_computation.128 | convolution fusion | flops 1342177280 | bytes 13369344 | tf_op jit(solution)/shard_map/dot_general | solution.py:21
  280.5 4.1 convolution_add_fusion.1
  284.7 3.8 fusion.72
  290.6 199.0 %all-reduce.3.cloned.1.call-done = bf16[32768,1,2,128]{3,2,1,0:T(2,128)(2,1)} async-done(((bf16[32768,1,2,128]{3,2,1,0:T(2,128)(2,1)}), bf16[32768,1,2,128]{3,2,1,0:T(2,128)(2,1)}) %all-reduce.3.cloned.1.call-update) | async-done | bytes 16777232
  489.7 2.6 constant_dynamic-slice_fusion
  492.2 32.6 %reduce-scatter.2.cloned.1.call-done = bf16[16,5120]{1,0:T(8,128)(2,1)} async-done(((bf16[128,5120]{1,0:T(8,128)(2,1)}), bf16[16,5120]{1,0:T(8,128)(2,1)}) %reduce-scatter.2.cloned.1.call-update) | async-done | bytes 163856 | tf_op jit(solution)/shard_map/reduce_scatter | solution.py:196
  (154 shorter events, 91.4 us)
Async XLA Ops:
  7.2 35.4 %copy-start = (bf16[5120,128]{1,0:T(8,128)(2,1)S(1)}, bf16[5120,128]{1,0:T(8,128)(2,1)}, u32[]{:S(2)}) copy-start(bf16[5120,128]{1,0:T(8,128)(2,1)} %param.14) | copy-start | bytes 3932164
  7.2 29.3 %all-gather.5.cloned.1.call-start = ((), (), s32[]{:S(2)}) async-start(), calls=%async_computation.2 | async-start | bytes 1474560 | tf_op jit(solution)/shard_map/all_gather | solution.py:101
  7.9 142.5 %all-gather.3.cloned.1.call-start = ((), (), s32[]{:S(2)}) async-start(), calls=%async_computation.1 | async-start | bytes 17825792 | tf_op jit(solution)/shard_map/all_gather | solution.py:131
  10.3 479.4 %all-reduce.3.cloned.1.call-start = ((), (), s32[]{:S(2)}) async-start(), calls=%async_computation.4 | async-start | bytes 33554432
  13.1 29.4 %copy-start.8 = (bf16[128,1024]{0,1:T(8,128)(2,1)}, bf16[128,1024]{0,1:T(8,128)(2,1)S(1)}, u32[]{:S(2)}) copy-start(bf16[128,1024]{0,1:T(8,128)(2,1)S(1)} %copy.42) | copy-start | bytes 786436
  36.5 6.1 %copy-start.1 = (bf16[128,5120]{1,0:T(8,128)(2,1)S(1)}, bf16[128,5120]{1,0:T(8,128)(2,1)}, u32[]{:S(2)}) copy-start(bf16[128,5120]{1,0:T(8,128)(2,1)} %all-gather.5.cloned.1.call-done) | copy-start | bytes 3932164
  42.5 1.3 copy-start.2
  154.8 37.5 %copy-start.4 = (bf16[128,1024]{1,0:T(8,128)(2,1)S(1)}, bf16[128,1024]{1,0:T(8,128)(2,1)}, u32[]{:S(2)}) copy-start(bf16[128,1024]{1,0:T(8,128)(2,1)} %param.19) | copy-start | bytes 786436
  192.7 0.7 copy-start.5
  269.1 1.1 copy-start.6
  269.1 255.7 %reduce-scatter.2.cloned.1.call-start = ((), (), s32[]{:S(2)}) async-start(), calls=%async_computation.3 | async-start | bytes 1474560 | tf_op jit(solution)/shard_map/reduce_scatter | solution.py:196
  280.5 4.1 copy-start.3
  280.5 4.1 copy-start.7
  284.6 3.9 copy-start.10
  284.6 5.1 copy-start.9
Sparse Core Ops, SparseCore 0:
  9.7 26.7 all-gather.4
  39.2 111.1 all-gather.2
  269.2 220.3 all-reduce.2
  492.5 32.2 reduce-scatter.1
where the time goes:
time: 533 us; the launch traced here: 531 us
  waiting for transfers between devices  361 us (68%)
  matrix products  110 us (21%)
  local copies, waits for them, and re-layouts  35.8 us (7%)
  between operations  15.3 us (3%)
  other arithmetic  7.64 us (1%)
    unnamed x5, waiting for transfers between devices  200 us
    all_gather x1, waiting for transfers between devices, on_device(): gathered = lax.all_gather(prefix_cache, 'seq', axis=0, tiled=True)  106 us
    reduce_scatter x1, waiting for transfers between devices, on_device(): lax.psum_scatter((contract(query_grad, query_weight) + contract(key_grad,...  32.6 us
    all_gather x1, waiting for transfers between devices, on_device(): segment = lax.all_gather(hidden, 'tp', axis=0, tiled=True)  23.1 us
    dot_general x9, matrix products, forward_block(): jnp.einsum('gjrk,kgd->rgjd', unnormed.astype(jnp.bfloat16), block_values,...  17.8 us
    dot_general x9, matrix products, backward_block(): jnp.einsum('rgjd,kgd->gjrk', out_grad, block_values, preferred_element_ty...  17.1 us
    dot_general x3, matrix products, contract(): lax.dot_general(grads, weight, (((1,), (1,)), ((), ())), preferred_elemen...  17.1 us
    dot_general x9, matrix products, forward_block(): jnp.einsum('rgjd,kgd->gjrk', queries, block_keys, preferred_element_type=...  13.6 us
  transfers between devices with their start and end apart: 4, of which 4 were waited for; matrix products, arithmetic and copies ran while one was open for 7% of the time, Pallas kernels for 0%

commit v1 on v0

v1 whole, which is shorter than its diff:
```python
import functools
import math

import jax
import jax.numpy as jnp
from jax import lax
from jax.experimental import pallas as pl
from jax.experimental.pallas import tpu as pltpu
from jax.sharding import PartitionSpec as P

HD = 128
RESP_LEN = 32
ROWS = 128
SLICE = 256
STAT_ROWS = 16
CHUNK = 2048
HALF = 1024
KEYS = 8192
WROWS = 1024
BLOCK = 1024
SCALE = HD ** -0.5
EXP2_SCALE = SCALE * math.log2(math.e)
NEG = -1.0e30
BF = jnp.bfloat16
F32 = jnp.float32
NT = (((1,), (1,)), ((), ()))
NN = (((1,), (0,)), ((), ()))
ANY = pl.BlockSpec(memory_space=pl.ANY)
VM = pl.BlockSpec(memory_space=pltpu.VMEM)
XG = [[a * 4 + b for a in range(4)] for b in range(4)]


def dot(a, b, dims):
    return lax.dot_general(a, b, dims, preferred_element_type=F32)


def move_tp(x, dz, dc):
    pairs = [(z * 2 + c, ((z + dz) % 4) * 2 + (c + dc) % 2) for z in range(4) for c in range(2)]
    return lax.ppermute(x, "tp", pairs)


def move_seq(x, dx, dy):
    pairs = [(a * 4 + b, ((a + dx) % 4) * 4 + (b + dy) % 4) for a in range(4) for b in range(4)]
    return lax.ppermute(x, "seq", pairs)


def ring_gather(a, b, move):
    pa, pb = move(a, 1), move(b, 1)
    nb, na = move(b, -1), move(a, -1)
    return [a, b, pa, pb, na, nb, move(pa, 1), move(nb, -1)]


def split3(v):
    hi = v.astype(BF).astype(F32)
    mid = (v - hi).astype(BF).astype(F32)
    return hi, mid, v - hi - mid


def stat_rows(first, second):
    rows = list(split3(first)) + list(split3(second))
    return jnp.concatenate(rows + [jnp.zeros((STAT_ROWS - 6, SLICE), F32)], axis=0).astype(BF)


def read_stats(rows):
    r = rows.astype(F32)
    return r[0:1] + r[1:2] + r[2:3], r[3:4] + r[4:5] + r[5:6]


def causal_mask(lens):
    key = lax.broadcasted_iota(jnp.int32, (ROWS, ROWS), 0)
    row = lax.broadcasted_iota(jnp.int32, (ROWS, ROWS), 1)
    member = lax.shift_right_logical(key, 5)
    length = jnp.where(member == 0, lens[0], jnp.where(member == 1, lens[1], jnp.where(member == 2, lens[2], lens[3])))
    live = (key & (RESP_LEN - 1)) < length
    return (member == lax.shift_right_logical(row, 5)) & (key <= row) & live


def grads_kernel(meta, cg_ref, out_ref):
    pos = lax.broadcasted_iota(jnp.int32, (ROWS, SLICE), 0)
    member = lax.shift_right_logical(pos, 5)
    length = jnp.where(member == 0, meta[4], jnp.where(member == 1, meta[5], jnp.where(member == 2, meta[6], meta[7])))
    live = (pos & (RESP_LEN - 1)) < length
    out_ref[0] = jnp.where(live, cg_ref[...], jnp.zeros_like(cg_ref))


def masked_grads(meta, context_grad):
    return pl.pallas_call(
        grads_kernel,
        grid_spec=pltpu.PrefetchScalarGridSpec(
            num_scalar_prefetch=1,
            grid=(4,),
            in_specs=[pl.BlockSpec((ROWS, SLICE), lambda i, m: (0, (m[1] + i) % 4))],
            out_specs=pl.BlockSpec((1, ROWS, SLICE), lambda i, m: (i, 0, 0)),
        ),
        out_shape=jax.ShapeDtypeStruct((4, ROWS, SLICE), BF),
        name="masked_grads",
    )(meta, context_grad)


def project_kernel(meta, *refs):
    pieces, (wq, wk, wv, og), (out, k_out, v_out), (seg, sem) = refs[:10], refs[10:14], refs[14:17], refs[17:]
    i = pl.program_id(0)

    @pl.when(i == 0)
    def _():
        z, c = meta[2], meta[3]
        half = seg.shape[1] // 2
        copies = []
        for rc in range(2):
            mine = pieces[rc * 5:rc * 5 + 5]
            for n, (dz, col, width) in enumerate(((0, 0, 2 * half), (3, 0, 2 * half), (1, 0, 2 * half), (2, 0, half), (2, half, half))):
                start = pl.multiple_of((((z + dz) & 3) * 2 + (c ^ rc)) * 16, 16)
                copies.append(pltpu.make_async_copy(mine[n], seg.at[pl.ds(start, 16), pl.ds(col, width)], sem.at[rc * 5 + n]))
        for copy in copies:
            copy.start()
        for copy in copies:
            copy.wait()
        k_out[...] = dot(seg[...], wk[...], NN).astype(BF)
        v_out[...] = dot(seg[...], wv[...], NN).astype(BF)

    q = dot(seg[...], wq[...], NN).astype(BF)
    out[0, :ROWS] = q
    mask = causal_mask([meta[4], meta[5], meta[6], meta[7]])
    lses, corrs = [], []
    for j in range(2):
        cols = slice(j * HD, (j + 1) * HD)
        s = jnp.where(mask, dot(k_out[...], q[:, cols], NT) * SCALE, NEG)
        top = jnp.max(s, axis=0, keepdims=True)
        p = jnp.where(mask, jnp.exp(s - top), 0.0)
        total = jnp.sum(p, axis=0, keepdims=True)
        dp = dot(v_out[...], og[0, :, cols], NT)
        lses.append(top + jnp.log(total))
        corrs.append(jnp.sum(p.astype(BF).astype(F32) * dp, axis=0, keepdims=True) / total)
    out[0, ROWS:] = stat_rows(jnp.concatenate(lses, axis=1), jnp.concatenate(corrs, axis=1))


def project(meta, pieces, wq, wk, wv, og_rel):
    d = wq.shape[0]
    return pl.pallas_call(
        project_kernel,
        grid_spec=pltpu.PrefetchScalarGridSpec(
            num_scalar_prefetch=1,
            grid=(4,),
            in_specs=[ANY] * 10 + [
                pl.BlockSpec((d, SLICE), lambda i, m: (0, (m[1] + i) % 4)),
                pl.BlockSpec((d, HD), lambda i, m: (0, 0)),
                pl.BlockSpec((d, HD), lambda i, m: (0, 0)),
                pl.BlockSpec((1, ROWS, SLICE), lambda i, m: (i, 0, 0)),
            ],
            out_specs=[
                pl.BlockSpec((1, ROWS + STAT_ROWS, SLICE), lambda i, m: (i, 0, 0)),
                pl.BlockSpec((ROWS, HD), lambda i, m: (0, 0)),
                pl.BlockSpec((ROWS, HD), lambda i, m: (0, 0)),
            ],
            scratch_shapes=[pltpu.VMEM((ROWS, d), BF), pltpu.SemaphoreType.DMA((10,))],
        ),
        out_shape=[
            jax.ShapeDtypeStruct((4, ROWS + STAT_ROWS, SLICE), BF),
            jax.ShapeDtypeStruct((ROWS, HD), BF),
            jax.ShapeDtypeStruct((ROWS, HD), BF),
        ],
        compiler_params=pltpu.CompilerParams(vmem_limit_bytes=24 << 20),
        cost_estimate=pl.CostEstimate(flops=2 * ROWS * d * 1280, bytes_accessed=d * 1280 * 2, transcendentals=0),
        name="project",
    )(meta, *pieces, wq, wk, wv, og_rel)


def worker_kernel(meta, *refs):
    q_in, og_in, kv_in = refs[:8], refs[8:16], refs[16:24]
    dq_out, ctx_out, q_all, og_all, a_hbm, ds_hbm = refs[24:30]
    qslot, ogslot, kv, p_all, ds_all, acc, dqt, mblk, m_ref, l_ref, sem_in, sem_kv, sem_out = refs[30:]
    blocks = KEYS // BLOCK

    kv_copies = [pltpu.make_async_copy(kv_in[n], kv.at[pl.ds(n * HALF, HALF)], sem_kv.at[n]) for n in range(8)]
    for r in range(4):
        code, place = meta[8 + r], meta[12 + r]
        for n in range(8):
            @pl.when(code == n)
            def _():
                pltpu.make_async_copy(q_in[n].at[place], qslot.at[r], sem_in.at[r]).start()
                pltpu.make_async_copy(og_in[n].at[place], ogslot.at[r], sem_in.at[4 + r]).start()
    for copy in kv_copies:
        copy.start()
    dq_out[...] = jnp.zeros_like(dq_out)
    ctx_out[...] = jnp.zeros_like(ctx_out)
    m_ref[...] = jnp.full_like(m_ref, NEG)
    l_ref[...] = jnp.zeros_like(l_ref)
    acc[...] = jnp.zeros_like(acc)
    dqt[...] = jnp.zeros_like(dqt)
    for r in range(4):
        pltpu.make_async_copy(q_in[0].at[0], qslot.at[r], sem_in.at[r]).wait()
        pltpu.make_async_copy(og_in[0].at[0], ogslot.at[r], sem_in.at[4 + r]).wait()
        for j in range(2):
            rows = slice(r * SLICE + j * HD, r * SLICE + (j + 1) * HD)
            cols = slice(j * HD, (j + 1) * HD)
            q_all[rows] = qslot[r, :ROWS, cols]
            og_all[rows] = ogslot[r, :, cols]
    for copy in kv_copies:
        copy.wait()

    def forward(b, _):
        keys = pl.ds(pl.multiple_of(b * BLOCK, BLOCK), BLOCK)
        kb = kv[keys, :HD]
        vt = kv[keys, HD:].T
        for r in range(4):
            rs = slice(r * SLICE, (r + 1) * SLICE)
            s = dot(kb, q_all[rs], NT)
            old = m_ref[:, rs]
            new = jnp.maximum(old, jnp.max(s, axis=0, keepdims=True))
            p = jnp.exp2((s - new) * EXP2_SCALE)
            factor = jnp.exp2((old - new) * EXP2_SCALE)
            l_ref[:, rs] = l_ref[:, rs] * factor + jnp.sum(p, axis=0, keepdims=True)
            pb = p.astype(BF)
            p_all[keys, rs] = pb
            acc[:, rs] = acc[:, rs] * factor + dot(vt, pb, NN)
            m_ref[:, rs] = new
            mblk[pl.ds(b, 1), rs] = new
        return 0

    lax.fori_loop(0, blocks, forward, 0)

    norms, corrs = [], []
    for r in range(4):
        rs = slice(r * SLICE, (r + 1) * SLICE)
        lse0, corr0 = read_stats(qslot[r, ROWS:])
        lse = m_ref[:, rs] * SCALE + jnp.log(l_ref[:, rs])
        top = jnp.maximum(lse, lse0)
        log_norm = top + jnp.log(jnp.exp(lse - top) + jnp.exp(lse0 - top))
        inv = jnp.exp(lse - log_norm) / l_ref[:, rs]
        ctx = acc[:, rs] * inv
        ogt = og_all[rs].astype(F32).T
        corr = jnp.sum(ogt * ctx, axis=0, keepdims=True) + corr0 * jnp.exp(lse0 - log_norm)
        ctx_rows = ctx.T
        spot = meta[16 + r]
        for j in range(2):
            ctx_out[spot, :, j * HD:(j + 1) * HD] = ctx_rows[j * HD:(j + 1) * HD].astype(BF)
        dq_out[spot, ROWS:] = stat_rows(log_norm, corr)
        norms.append(inv)
        corrs.append(corr)

    def backward(b, _):
        keys = pl.ds(pl.multiple_of(b * BLOCK, BLOCK), BLOCK)
        kt = kv[keys, :HD].T
        vb = kv[keys, HD:]
        for r in range(4):
            rs = slice(r * SLICE, (r + 1) * SLICE)
            dp = dot(vb, og_all[rs], NT)
            factor = jnp.exp2((mblk[pl.ds(b, 1), rs] - m_ref[:, rs]) * EXP2_SCALE) * norms[r]
            a = p_all[keys, rs].astype(F32) * factor
            ds = (a * (dp - corrs[r])).astype(BF)
            p_all[keys, rs] = a.astype(BF)
            ds_all[keys, rs] = ds
            dqt[:, rs] += dot(kt, ds, NN)
        pltpu.make_async_copy(p_all.at[keys], a_hbm.at[keys], sem_out.at[0, b]).start()
        pltpu.make_async_copy(ds_all.at[keys], ds_hbm.at[keys], sem_out.at[1, b]).start()
        return 0

    lax.fori_loop(0, blocks, backward, 0)
    for r in range(4):
        rows = (dqt[:, r * SLICE:(r + 1) * SLICE] * SCALE).T
        for j in range(2):
            dq_out[meta[16 + r], :ROWS, j * HD:(j + 1) * HD] = rows[j * HD:(j + 1) * HD].astype(BF)
    for b in range(blocks):
        keys = pl.ds(b * BLOCK, BLOCK)
        pltpu.make_async_copy(p_all.at[keys], a_hbm.at[keys], sem_out.at[0, b]).wait()
        pltpu.make_async_copy(ds_all.at[keys], ds_hbm.at[keys], sem_out.at[1, b]).wait()


def work(meta, q_parts, og_parts, kv_parts):
    blocks = KEYS // BLOCK
    return pl.pallas_call(
        worker_kernel,
        in_specs=[pl.BlockSpec(memory_space=pltpu.SMEM)] + [ANY] * 24,
        out_specs=[VM, VM, VM, VM, ANY, ANY],
        out_shape=[
            jax.ShapeDtypeStruct((16, ROWS + STAT_ROWS, SLICE), BF),
            jax.ShapeDtypeStruct((16, ROWS, SLICE), BF),
            jax.ShapeDtypeStruct((WROWS, HD), BF),
            jax.ShapeDtypeStruct((WROWS, HD), BF),
            jax.ShapeDtypeStruct((KEYS, WROWS), BF),
            jax.ShapeDtypeStruct((KEYS, WROWS), BF),
        ],
        scratch_shapes=[
            pltpu.VMEM((4, ROWS + STAT_ROWS, SLICE), BF),
            pltpu.VMEM((4, ROWS, SLICE), BF),
            pltpu.VMEM((KEYS, SLICE), BF),
            pltpu.VMEM((KEYS, WROWS), BF),
            pltpu.VMEM((KEYS, WROWS), BF),
            pltpu.VMEM((HD, WROWS), F32),
            pltpu.VMEM((HD, WROWS), F32),
            pltpu.VMEM((blocks, WROWS), F32),
            pltpu.VMEM((1, WROWS), F32),
            pltpu.VMEM((1, WROWS), F32),
            pltpu.SemaphoreType.DMA((8,)),
            pltpu.SemaphoreType.DMA((8,)),
            pltpu.SemaphoreType.DMA((2, blocks)),
        ],
        compiler_params=pltpu.CompilerParams(vmem_limit_bytes=58 << 20),
        cost_estimate=pl.CostEstimate(flops=8 * WROWS * KEYS * HD, bytes_accessed=40 << 20, transcendentals=WROWS * KEYS),
        name="attention",
    )(meta, *q_parts, *og_parts, *kv_parts)


def cache_grad_kernel(a_ref, ds_ref, q_ref, og_ref, out_a, out_b):
    dk = dot(ds_ref[...], q_ref[...], NN) * SCALE
    dv = dot(a_ref[...], og_ref[...], NN)
    both = jnp.concatenate([dk, dv], axis=1).astype(BF)
    i = pl.program_id(0)

    @pl.when(i < 2)
    def _():
        out_a[...] = both

    @pl.when(i >= 2)
    def _():
        out_b[...] = both


def cache_grad(chunk, a, ds, q_all, og_all):
    size = CHUNK // 4
    return pl.pallas_call(
        cache_grad_kernel,
        grid=(4,),
        in_specs=[
            pl.BlockSpec((size, WROWS), lambda i: (chunk * 4 + i, 0)),
            pl.BlockSpec((size, WROWS), lambda i: (chunk * 4 + i, 0)),
            pl.BlockSpec((WROWS, HD), lambda i: (0, 0)),
            pl.BlockSpec((WROWS, HD), lambda i: (0, 0)),
        ],
        out_specs=[
            pl.BlockSpec((size, SLICE), lambda i: (jnp.minimum(i, 1), 0)),
            pl.BlockSpec((size, SLICE), lambda i: (jnp.maximum(i - 2, 0), 0)),
        ],
        out_shape=[jax.ShapeDtypeStruct((HALF, SLICE), BF)] * 2,
        compiler_params=pltpu.CompilerParams(vmem_limit_bytes=24 << 20),
        cost_estimate=pl.CostEstimate(flops=4 * CHUNK * WROWS * HD, bytes_accessed=9 << 20, transcendentals=0),
        name="cache_grad",
    )(a, ds, q_all, og_all)


def hidden_kernel(meta, *refs):
    dq_in, (qs, og, k, v, wq, wk, wv), (out,), (dq_s, dk_s, dv_s, part) = refs[:4], refs[4:11], refs[11:12], refs[12:]
    i = pl.program_id(0)

    @pl.when(i == 0)
    def _():
        mask = causal_mask([meta[4], meta[5], meta[6], meta[7]])
        dk = jnp.zeros((ROWS, HD), F32)
        dv = jnp.zeros((ROWS, HD), F32)
        for n in range(4):
            rel = (4 - n) % 4
            log_norm, corr = read_stats(dq_in[n][ROWS:])
            start = pl.multiple_of(((meta[1] + rel) & 3) * SLICE, SLICE)
            for j in range(2):
                cols = slice(j * HD, (j + 1) * HD)
                qj, ogj = qs[rel, :ROWS, cols], og[rel, :, cols]
                s = dot(k[...], qj, NT) * SCALE
                a = jnp.where(mask, jnp.exp(jnp.where(mask, s - log_norm[:, cols], 0.0)), 0.0)
                ds = (a * (dot(v[...], ogj, NT) - corr[:, cols]))
                dsb = ds.astype(BF)
                dk += dot(dsb, qj, NN)
                dv += dot(a.astype(BF), ogj, NN)
                dq = dot(ds.T.astype(BF), k[...], NN) * SCALE
                dq_s[:, pl.ds(start + j * HD, HD)] = (dq_in[n][:ROWS, cols].astype(F32) + dq).astype(BF)
        dk_s[...] = (dk * SCALE).astype(BF)
        dv_s[...] = dv.astype(BF)

    part[...] = dot(dq_s[...], wq[...], NT) + dot(dk_s[...], wk[...], NT) + dot(dv_s[...], wv[...], NT)
    z, c = meta[2], meta[3]
    for rc in range(2):
        for dz in range(4):
            start = pl.multiple_of((((z + dz) & 3) * 2 + (c ^ rc)) * 16, 16)
            out[rc, dz] = part[pl.ds(start, 16), :].astype(BF)


def hidden_grad_parts(meta, dq_parts, q_rel, og_rel, k, v, wq, wk, wv):
    d = wq.shape[0]
    size = 512
    full = lambda shape: pl.BlockSpec(shape, lambda i, m: (0,) * len(shape))
    return pl.pallas_call(
        hidden_kernel,
        grid_spec=pltpu.PrefetchScalarGridSpec(
            num_scalar_prefetch=1,
            grid=(d // size,),
            in_specs=[full((ROWS + STAT_ROWS, SLICE))] * 4 + [
                full((4, ROWS + STAT_ROWS, SLICE)),
                full((4, ROWS, SLICE)),
                full((ROWS, HD)),
                full((ROWS, HD)),
                pl.BlockSpec((size, 1024), lambda i, m: (i, 0)),
                pl.BlockSpec((size, HD), lambda i, m: (i, 0)),
                pl.BlockSpec((size, HD), lambda i, m: (i, 0)),
            ],
            out_specs=pl.BlockSpec((2, 4, 16, size), lambda i, m: (0, 0, 0, i)),
            scratch_shapes=[
                pltpu.VMEM((ROWS, 1024), BF),
                pltpu.VMEM((ROWS, HD), BF),
                pltpu.VMEM((ROWS, HD), BF),
                pltpu.VMEM((ROWS, size), F32),
            ],
        ),
        out_shape=jax.ShapeDtypeStruct((2, 4, 16, d), BF),
        compiler_params=pltpu.CompilerParams(vmem_limit_bytes=24 << 20),
        cost_estimate=pl.CostEstimate(flops=2 * ROWS * d * 1280, bytes_accessed=d * 1280 * 2, transcendentals=0),
        name="hidden_grad",
    )(meta, *dq_parts, q_rel, og_rel, k, v, wq, wk, wv)


def context_kernel(meta, *refs):
    ctx_in, (qs, k, v, dq0, dq1, dq2, dq3), (out,) = refs[:4], refs[4:11], refs[11:]
    stats = (dq0, dq1, dq2, dq3)
    mask = causal_mask([meta[4], meta[5], meta[6], meta[7]])
    row = lax.broadcasted_iota(jnp.int32, (ROWS, HD), 0)
    member = lax.shift_right_logical(row, 5)
    length = jnp.where(member == 0, meta[4], jnp.where(member == 1, meta[5], jnp.where(member == 2, meta[6], meta[7])))
    live = (row & (RESP_LEN - 1)) < length
    for n in range(4):
        rel = (4 - n) % 4
        log_norm, _ = read_stats(stats[n][ROWS:])
        start = pl.multiple_of(((meta[1] + rel) & 3) * SLICE, SLICE)
        for j in range(2):
            cols = slice(j * HD, (j + 1) * HD)
            s = dot(k[...], qs[rel, :ROWS, cols], NT) * SCALE
            a = jnp.where(mask, jnp.exp(jnp.where(mask, s - log_norm[:, cols], 0.0)), 0.0)
            own = dot(a.T.astype(BF), v[...], NN)
            total = jnp.where(live, ctx_in[n][:, cols].astype(F32) + own, 0.0)
            out[:, pl.ds(start + j * HD, HD)] = total.astype(BF)


def finish_context(meta, ctx_parts, q_rel, k, v, dq_parts):
    return pl.pallas_call(
        context_kernel,
        in_specs=[pl.BlockSpec(memory_space=pltpu.SMEM)] + [VM] * 11,
        out_specs=VM,
        out_shape=jax.ShapeDtypeStruct((ROWS, 1024), BF),
        compiler_params=pltpu.CompilerParams(vmem_limit_bytes=16 << 20),
        name="context",
    )(meta, *ctx_parts, q_rel, k, v, *dq_parts)


def send_back(dense):
    shape = dense.shape
    mine = lax.psum_scatter(dense.reshape(-1, SLICE), "seq", scatter_dimension=0, tiled=True, axis_index_groups=XG)
    mine = mine.reshape(4, shape[1], SLICE)
    return [mine[0]] + [move_seq(mine[n], 0, n) for n in (1, 2, 3)]


def spread(parts):
    here = [parts[0]] + [move_seq(parts[n], 0, n) for n in (1, 2, 3)]
    a = jnp.stack([here[0], here[1]])
    b = jnp.stack([here[2], here[3]])
    return ring_gather(a, b, lambda v, d: move_seq(v, d, 0))


def on_device(hidden, wq, wk, wv, prefix_cache, owner_prompt, response_length, context_grad):
    seq, tp = lax.axis_index("seq"), lax.axis_index("tp")
    x, y, z, c = seq // 4, seq % 4, tp // 2, tp % 2
    place = jnp.stack([x, y, z, c]).astype(jnp.int32)
    base = jnp.concatenate([place, response_length])

    prompts = lax.all_gather(owner_prompt, "seq", axis=0, tiled=True)
    owners = jnp.arange(16, dtype=jnp.int32)
    match = prompts == x
    rank = jnp.sum(match[None, :] & (owners[None, :] < owners[:, None]), axis=1)
    chosen = match[None, :] & (rank[None, :] == jnp.arange(4)[:, None])
    sel = jnp.sum(jnp.where(chosen, owners[None, :], 0), axis=1).astype(jnp.int32)
    sel_x, sel_y = sel // 4, sel % 4
    dx, dy = (x - sel_x) % 4, (y - sel_y) % 4
    ring_at = jnp.where(dx == 0, 0, jnp.where(dx == 1, 1, jnp.where(dx == 3, 2, 3)))
    code = ring_at * 2 + dy // 2
    spot = sel_x * 4 + (sel_y - y) % 4
    meta = jnp.concatenate([base, code, dy % 2, spot]).astype(jnp.int32)

    cache = prefix_cache.reshape(CHUNK, SLICE)
    kv_parts = ring_gather(cache[:HALF], cache[HALF:], lambda v, d: move_seq(v, 0, d))

    og_rel = masked_grads(base, context_grad)
    og_parts = spread([og_rel[n] for n in range(4)])

    half = hidden.shape[1] // 2
    before, after = move_tp(hidden, 1, 0), move_tp(hidden, -1, 0)
    group = [hidden, before, after, move_tp(before[:, :half], 1, 0), move_tp(after[:, half:], -1, 0)]
    pieces = group + [move_tp(v, 0, 1) for v in group]
    q_rel, k, v = project(base, pieces, wq, wk, wv, og_rel)
    q_parts = spread([q_rel[n] for n in range(4)])

    dq_dense, ctx_dense, q_all, og_all, a, ds = work(meta, q_parts, og_parts, kv_parts)
    dq_parts = send_back(dq_dense)

    grad = functools.partial(cache_grad, a=a, ds=ds, q_all=q_all, og_all=og_all)
    far_a, far_b = grad(3)
    got_a, got_b = move_seq(far_a, 0, 1), move_seq(far_b, 0, -1)
    prev_a, prev_b = grad(1)
    next_a, next_b = grad(2)
    own_a, own_b = grad(0)
    add = lambda *terms: sum(t.astype(F32) for t in terms).astype(BF)
    from_prev_b = move_seq(next_b, 0, 1)
    from_next_a = move_seq(prev_a, 0, -1)
    from_prev_a = move_seq(add(next_a, got_a), 0, 1)
    from_next_b = move_seq(add(prev_b, got_b), 0, -1)
    prefix_grad = jnp.concatenate([add(own_a, from_prev_a, from_next_a), add(own_b, from_prev_b, from_next_b)])
    prefix_grad = prefix_grad.reshape(CHUNK, 1, 2, HD)

    parts = hidden_grad_parts(base, dq_parts, q_rel, og_rel, k, v, wq, wk, wv)
    pair = add(parts[0], move_tp(parts[1], 0, 1))
    hidden_grad = add(pair[0], *[move_tp(pair[n], n, 0) for n in (1, 2, 3)])

    ctx_parts = send_back(ctx_dense)
    context = finish_context(base, ctx_parts, q_rel, k, v, dq_parts)
    return context, hidden_grad, prefix_grad


def solution(mesh):
    return jax.shard_map(
        on_device,
        mesh=mesh,
        in_specs=(
            P(("seq", "tp"), None),
            P(None, "tp"),
            P(None, "tp"),
            P(None, "tp"),
            P("seq", "tp", None, None),
            P("seq"),
            P("seq"),
            P("seq", "tp"),
        ),
        out_specs=(P("seq", "tp"), P(("seq", "tp"), None), P("seq", "tp", None, None)),
        check_vma=False,
    )
```

time: 533 us -> 277 us (0.52)
  waiting for transfers between devices: 361 us -> 30.5 us
  matrix products: 110 us -> 0 us
  Pallas kernels: 0 us -> 92.4 us
  starting transfers between devices: 0.34 us -> 74.5 us
  blocking collectives: 0 us -> 15.3 us
    unnamed x5 -> x2, waiting for transfers between devices: 200 us -> 0.03 us
    all_gather x2 -> x0, waiting for transfers between devices: 129 us -> none  [the longest x1 106 us: on_device(): gathered = lax.all_gather(prefix_cache, 'seq', axis=0, tiled=True)]
    dot_general x66 -> x0, matrix products: 110 us -> none  [the longest x9 17.8 us: forward_block(): jnp.einsum('gjrk,kgd->rgjd', unnormed.astype(jnp.bfloat16), block_values,...]
    pallas_call x0 -> x9, Pallas kernels: none -> 92.4 us  [the longest x1 47.2 us: work(): pl.pallas_call(worker_kernel, in_specs=[pl.BlockSpec(memory_space=pltpu.S...]
    ppermute x0 -> x49, starting transfers between devices: none -> 74.5 us  [the longest x36 62.9 us: move_seq(): return lax.ppermute(x, 'seq', pairs)]
    reduce_scatter x1 -> x2, waiting for transfers between devices: 32.6 us -> 0.01 us  [send_back(): lax.psum_scatter(dense.reshape(-1, SLICE), 'seq', scatter_dimension=0, ti...]
    ppermute x0 -> x49, waiting for transfers between devices: none -> 30.5 us  [the longest x36 25.3 us: move_seq(): return lax.ppermute(x, 'seq', pairs)]
    unnamed x29 -> x95, local copies, waits for them, and re-layouts: 8.32 us -> 25.4 us
  transfers between devices with their start and end apart: 4 -> 51, of which waited for: 4 -> 9; matrix products, arithmetic and copies ran while one was open for 7% -> 9% of each run, Pallas kernels for 0% -> 16%
where the time goes in v1:
time: 277 us; the launch traced here: 275 us
  Pallas kernels  92.4 us (33%)
  starting transfers between devices  74.5 us (27%)
  local copies, waits for them, and re-layouts  35.5 us (13%)
  waiting for transfers between devices  30.5 us (11%)
  blocking collectives  15.3 us (6%)
  between operations  15.3 us (6%)
  other arithmetic  11.1 us (4%)
    ppermute x36, starting transfers between devices, move_seq(): return lax.ppermute(x, 'seq', pairs)  62.9 us
    pallas_call x1, Pallas kernels, work(): pl.pallas_call(worker_kernel, in_specs=[pl.BlockSpec(memory_space=pltpu.S...  47.2 us
    unnamed x95, local copies, waits for them, and re-layouts  25.4 us
    ppermute x36, waiting for transfers between devices, move_seq(): return lax.ppermute(x, 'seq', pairs)  25.3 us
    pallas_call x4, Pallas kernels, cache_grad(): pl.pallas_call(cache_grad_kernel, grid=(4,), in_specs=[pl.BlockSpec((size...  21.6 us
    unnamed x1, blocking collectives  15.3 us
    ppermute x13, starting transfers between devices, move_tp(): return lax.ppermute(x, 'tp', pairs)  11.6 us
    convert_element_type x6, other arithmetic, on_device(): add = lambda *terms: sum((t.astype(F32) for t in terms)).astype(BF)  10.6 us
  transfers between devices with their start and end apart: 51, of which 9 were waited for; matrix products, arithmetic and copies ran while one was open for 9% of the time, Pallas kernels for 16%

profile of v1, /device:TPU:0, one launch (start us, length us, event | category | flops | bytes accessed | tf_op | source)
XLA Modules:
  0.0 274.6 jit_solution(4915309310083669436)
XLA Ops:
  7.2 4.2 %collective-permute-start.1 = (bf16[16,5120]{1,0:T(8,128)(2,1)}, bf16[16,5120]{1,0:T(8,128)(2,1)S(1)}, u32[]{:S(2)}, u32[]{:S(2)}) collective-permute-start(bf16[16,5120]{1,0:T(8,128)(2,1)} %refs_0_.1), channel_id=1, source_target_pairs={{0,6},{1,7},{2,0},{3,1},{4,2},{5,3},{6,4},{7,5},{8,14},{9,15},{10,... | collective-permute-start | bytes 491528 | tf_op jit(solution)/shard_map/ppermute | solution.py:39
  12.7 3.6 %masked_grads.1.refs_13_.refs_5_ = bf16[4,128,256]{2,1,0:T(8,128)(2,1)} custom-call(s32[8]{0:T(128)} %concatenate.10.meta, bf16[128,1024]{1,0:T(8,128)(2,1)} %cg_ref.1), custom_call_target="tpu_custom_call" | custom-call | tf_op jit(solution)/shard_map/masked_grads/pallas_call | solution.py:87
  26.2 15.3 %all-reduce = s32[16]{0:T(128)S(1)} all-reduce(s32[16]{0:T(128)S(1)} %dynamic-update-slice), channel_id=1, replica_groups=mesh['seq'=16,'tp'=8] {'seq'}, use_global_device_ids=true, to_apply=%add | all-reduce | flops 16 | bytes 128
  42.6 3.3 %collective-permute-start.3 = (bf16[16,2560]{1,0:T(8,128)(2,1)S(1)}, bf16[16,2560]{1,0:T(8,128)(2,1)S(1)}, u32[]{:S(2)}, u32[]{:S(2)}) collective-permute-start(bf16[16,2560]{1,0:T(8,128)(2,1)S(1)} %slice.121), channel_id=1, source_target_pairs={{0,6},{1,7},{2,0},{3,1},{4,2},{5,3},{6,4},{7,5},{8,14},{9,15},{10,... | collective-permute-start | bytes 245768 | tf_op jit(solution)/shard_map/ppermute | solution.py:39
  58.2 4.0 %copy-done.1 = bf16[5120,1024]{1,0:T(8,128)(2,1)S(1)} copy-done((bf16[5120,1024]{1,0:T(8,128)(2,1)S(1)}, bf16[5120,1024]{1,0:T(8,128)(2,1)}, u32[]{:S(2)}) %copy-start.1) | copy-done | bytes 10485784
  64.0 8.1 %project.1 = (bf16[4,144,256]{2,1,0:T(8,128)(2,1)S(1)}, bf16[128,128]{1,0:T(8,128)(2,1)S(1)}, bf16[128,128]{1,0:T(8,128)(2,1)S(1)}) custom-call(s32[8]{0:T(128)S(1)} %copy-done.24, bf16[16,5120]{1,0:T(8,128)(2,1)S(1)} %copy-done.19, bf16[16,5120]{1,0:T(8,128)(2,1)S(1)} %collective-permute-done.refs_1_, bf16[16,5120]{1,0:T(8,128)(2,1)S(1)} %collective-permute-done.1.refs_2_, ...), custom_call_target="tpu_custom_call" | custom-call | flops 1677721600 | bytes 13107200 | tf_op jit(solution)/shard_map/project/pallas_call | solution.py:139
  81.5 10.5 %collective-permute-start.11 = (bf16[144,256]{1,0:T(8,128)(2,1)S(1)}, bf16[144,256]{1,0:T(8,128)(2,1)S(1)}, u32[]{:S(2)}, u32[]{:S(2)}) collective-permute-start(bf16[144,256]{1,0:T(8,128)(2,1)S(1)} %get-tuple-element.58), channel_id=1, source_target_pairs={{0,24},{8,0},{16,8},{24,16},{32,56},{40,32},{48,40},{56,48},{64,88... | collective-permute-start | bytes 221192 | tf_op jit(solution)/shard_map/ppermute | solution.py:44
  92.1 8.4 %collective-permute-done.11 = bf16[144,256]{1,0:T(8,128)(2,1)S(1)} collective-permute-done((bf16[144,256]{1,0:T(8,128)(2,1)S(1)}, bf16[144,256]{1,0:T(8,128)(2,1)S(1)}, u32[]{:S(2)}, u32[]{:S(2)}) %collective-permute-start.11) | collective-permute-done | bytes 73760 | tf_op jit(solution)/shard_map/ppermute | solution.py:44
  102.1 4.0 %collective-permute-done.9 = bf16[144,256]{1,0:T(8,128)(2,1)S(1)} collective-permute-done((bf16[144,256]{1,0:T(8,128)(2,1)S(1)}, bf16[144,256]{1,0:T(8,128)(2,1)S(1)}, u32[]{:S(2)}, u32[]{:S(2)}) %collective-permute-start.9) | collective-permute-done | bytes 73760 | tf_op jit(solution)/shard_map/ppermute | solution.py:44
  118.6 4.2 %collective-permute-done.12.refs_2_ = bf16[2,144,256]{2,1,0:T(8,128)(2,1)} collective-permute-done((bf16[2,144,256]{2,1,0:T(8,128)(2,1)S(1)}, bf16[2,144,256]{2,1,0:T(8,128)(2,1)}, u32[]{:S(2)}, u32[]{:S(2)}) %collective-permute-start.12) | collective-permute-done | bytes 147488 | tf_op jit(solution)/shard_map/ppermute | solution.py:44
  122.7 3.4 %collective-permute-start.17 = (bf16[2,144,256]{2,1,0:T(8,128)(2,1)}, bf16[2,144,256]{2,1,0:T(8,128)(2,1)}, u32[]{:S(2)}, u32[]{:S(2)}) collective-permute-start(bf16[2,144,256]{2,1,0:T(8,128)(2,1)} %collective-permute-done.15.refs_5_), channel_id=1, source_target_pairs={{0,96},{8,104},{16,112},{24,120},{32,0},{40,8},{48,16},{56,24},{64... | collective-permute-start | bytes 442376 | tf_op jit(solution)/shard_map/ppermute | solution.py:44
  129.4 47.2 %attention.1 = (bf16[16,144,256]{2,1,0:T(8,128)(2,1)}, bf16[16,128,256]{2,1,0:T(8,128)(2,1)}, bf16[1024,128]{1,0:T(8,128)(2,1)}, bf16[1024,128]{1,0:T(8,128)(2,1...) custom-call(s32[20]{0:T(128)} %concatenate.11.meta, bf16[2,144,256]{2,1,0:T(8,128)(2,1)} %copy-done.32, ...), custom_call_target="tpu_custom_call" | custom-call | flops 8589934592 | bytes 41943040 | tf_op jit(solution)/shard_map/attention/pallas_call | solution.py:271
  177.6 5.8 %copy-done = bf16[8192,1024]{1,0:T(8,128)(2,1)S(1)} copy-done((bf16[8192,1024]{1,0:T(8,128)(2,1)S(1)}, bf16[8192,1024]{1,0:T(8,128)(2,1)}, u32[]{:S(2)}) %copy-start) | copy-done | bytes 16777240
  183.4 5.8 %cache_grad.6 = (bf16[1024,256]{1,0:T(8,128)(2,1)}, bf16[1024,256]{1,0:T(8,128)(2,1)}) custom-call(bf16[8192,1024]{1,0:T(8,128)(2,1)S(1)} %copy-done, bf16[8192,1024]{1,0:T(8,128)(2,1)} %get-tuple-element.26.ds_ref, bf16[1024,128]{1,0:T(8,128)(2,1)S(1)} %copy-done.7, bf16[1024,128]{1,0:T(8,128)(2,1)S(1)} %copy-done.8), custom_call_target="tpu_custom_call" | custom-call | flops 1073741824 | bytes 9437184 | tf_op jit(solution)/shard_map/cache_grad/pallas_call | solution.py:321
  191.7 5.5 %cache_grad.7 = (bf16[1024,256]{1,0:T(8,128)(2,1)}, bf16[1024,256]{1,0:T(8,128)(2,1)S(1)}) custom-call(bf16[8192,1024]{1,0:T(8,128)(2,1)S(1)} %copy-done, bf16[8192,1024]{1,0:T(8,128)(2,1)} %get-tuple-element.26.ds_ref, bf16[1024,128]{1,0:T(8,128)(2,1)S(1)} %copy-done.7, bf16[1024,128]{1,0:T(8,128)(2,1)S(1)} %copy-done.8), custom_call_target="tpu_custom_call" | custom-call | flops 1073741824 | bytes 9437184 | tf_op jit(solution)/shard_map/cache_grad/pallas_call | solution.py:321
  198.1 5.5 %cache_grad.5 = (bf16[1024,256]{1,0:T(8,128)(2,1)S(1)}, bf16[1024,256]{1,0:T(8,128)(2,1)}) custom-call(bf16[8192,1024]{1,0:T(8,128)(2,1)S(1)} %copy-done, bf16[8192,1024]{1,0:T(8,128)(2,1)} %get-tuple-element.26.ds_ref, bf16[1024,128]{1,0:T(8,128)(2,1)S(1)} %copy-done.7, bf16[1024,128]{1,0:T(8,128)(2,1)S(1)} %copy-done.8), custom_call_target="tpu_custom_call" | custom-call | flops 1073741824 | bytes 9437184 | tf_op jit(solution)/shard_map/cache_grad/pallas_call | solution.py:321
  204.4 4.8 %cache_grad.4 = (bf16[1024,256]{1,0:T(8,128)(2,1)S(1)}, bf16[1024,256]{1,0:T(8,128)(2,1)S(1)}) custom-call(bf16[8192,1024]{1,0:T(8,128)(2,1)S(1)} %copy-done, bf16[8192,1024]{1,0:T(8,128)(2,1)} %get-tuple-element.26.ds_ref, bf16[1024,128]{1,0:T(8,128)(2,1)S(1)} %copy-done.7, bf16[1024,128]{1,0:T(8,128)(2,1)S(1)} %copy-done.8), custom_call_target="tpu_custom_call" | custom-call | flops 1073741824 | bytes 9437184 | tf_op jit(solution)/shard_map/cache_grad/pallas_call | solution.py:321
  217.1 3.3 %collective-permute-start.38 = (bf16[144,256]{1,0:T(8,128)(2,1)S(1)}, bf16[144,256]{1,0:T(8,128)(2,1)S(1)}, u32[]{:S(2)}, u32[]{:S(2)}) collective-permute-start(bf16[144,256]{1,0:T(8,128)(2,1)S(1)} %get-tuple-element.53), channel_id=1, source_target_pairs={{0,24},{8,0},{16,8},{24,16},{32,56},{40,32},{48,40},{56,48},{64,88... | collective-permute-start | bytes 221192 | tf_op jit(solution)/shard_map/ppermute | solution.py:44
  222.8 3.3 %collective-permute-done.38.refs_10_.refs_3_ = bf16[144,256]{1,0:T(8,128)(2,1)S(1)} collective-permute-done((bf16[144,256]{1,0:T(8,128)(2,1)S(1)}, bf16[144,256]{1,0:T(8,128)(2,1)S(1)}, u32[]{:S(2)}, u32[]{:S(2)}) %collective-permute-start.38) | collective-permute-done | bytes 73760 | tf_op jit(solution)/shard_map/ppermute | solution.py:44
  226.1 3.8 %collective-permute-start.48 = (bf16[1024,256]{1,0:T(8,128)(2,1)S(1)}, bf16[1024,256]{1,0:T(8,128)(2,1)S(1)}, u32[]{:S(2)}, u32[]{:S(2)}) collective-permute-start(bf16[1024,256]{1,0:T(8,128)(2,1)S(1)} %copy-done.28), channel_id=1, source_target_pairs={{0,24},{8,0},{16,8},{24,16},{32,56},{40,32},{48,40},{56,48},{64,88... | collective-permute-start | bytes 1572872 | tf_op jit(solution)/shard_map/ppermute | solution.py:44
  230.2 4.0 %copy-done.2 = bf16[5120,1024]{1,0:T(8,128)(2,1)S(1)} copy-done((bf16[5120,1024]{1,0:T(8,128)(2,1)S(1)}, bf16[5120,1024]{1,0:T(8,128)(2,1)}, u32[]{:S(2)}) %copy-start.2) | copy-done | bytes 10485784
  234.3 8.6 %hidden_grad.1 = bf16[2,4,16,5120]{3,2,1,0:T(8,128)(2,1)S(1)} custom-call(s32[8]{0:T(128)S(1)} %copy-done.24, bf16[144,256]{1,0:T(8,128)(2,1)S(1)} %get-tuple-element.56.refs_7_.refs_0_, bf16[144,256]{1,0:T(8,128)(2,1)S(1)} %collective-permute-done.36.refs_8_.refs_1_, bf16[144,256]{1,0:T(8,128)(2,1)S(1)} %collective-permute-done.37.refs_9_.refs_2_, ...), custom_call_target="tpu_custom_call" | custom-call | flops 1677721600 | bytes 13107200 | tf_op jit(solution)/shard_map/hidden_grad/pallas_call | solution.py:380
  255.6 3.2 %collective-permute-start.42 = (bf16[16,5120]{1,0:T(8,128)(2,1)}, bf16[16,5120]{1,0:T(8,128)(2,1)}, u32[]{:S(2)}, u32[]{:S(2)}) collective-permute-start(bf16[16,5120]{1,0:T(8,128)(2,1)} %get-tuple-element.51), channel_id=1, source_target_pairs={{0,6},{1,7},{2,0},{3,1},{4,2},{5,3},{6,4},{7,5},{8,14},{9,15},{10,... | collective-permute-start | bytes 491528 | tf_op jit(solution)/shard_map/ppermute | solution.py:39
  260.0 3.2 %context.1 = bf16[128,1024]{1,0:T(8,128)(2,1)} custom-call(s32[8]{0:T(128)S(1)} %copy-done.24, bf16[128,256]{1,0:T(8,128)(2,1)S(1)} %get-tuple-element.64.refs_0_, bf16[128,256]{1,0:T(8,128)(2,1)S(1)} %collective-permute-done.33.refs_1_, bf16[128,256]{1,0:T(8,128)(2,1)S(1)} %collective-permute-done.34.refs_2_, ...), custom_call_target="tpu_custom_call" | custom-call | tf_op jit(solution)/shard_map/context/pallas_call | solution.py:431
  (214 shorter events, 86.2 us)
Async XLA Ops:
  7.2 208.9 %reduce-scatter.5.cloned.1.call-start = ((), (), s32[]{:S(2)}) async-start(), calls=%async_computation.3 | async-start | bytes 1474560 | tf_op jit(solution)/shard_map/reduce_scatter | solution.py:443
  7.2 35.0 %collective-permute-start.1 = (bf16[16,5120]{1,0:T(8,128)(2,1)}, bf16[16,5120]{1,0:T(8,128)(2,1)S(1)}, u32[]{:S(2)}, u32[]{:S(2)}) collective-permute-start(bf16[16,5120]{1,0:T(8,128)(2,1)} %refs_0_.1), channel_id=1, source_target_pairs={{0,6},{1,7},{2,0},{3,1},{4,2},{5,3},{6,4},{7,5},{8,14},{9,15},{10,... | collective-permute-start | bytes 491528 | tf_op jit(solution)/shard_map/ppermute | solution.py:39
  11.4 31.2 %collective-permute-start = (bf16[16,5120]{1,0:T(8,128)(2,1)}, bf16[16,5120]{1,0:T(8,128)(2,1)S(1)}, u32[]{:S(2)}, u32[]{:S(2)}) collective-permute-start(bf16[16,5120]{1,0:T(8,128)(2,1)} %refs_0_.1), channel_id=1, source_target_pairs={{0,2},{1,3},{2,4},{3,5},{4,6},{5,7},{6,0},{7,1},{8,10},{9,11},{10,... | collective-permute-start | bytes 491528 | tf_op jit(solution)/shard_map/ppermute | solution.py:39
  11.4 34.7 %collective-permute-start.4 = (bf16[16,5120]{1,0:T(8,128)(2,1)}, bf16[16,5120]{1,0:T(8,128)(2,1)S(1)}, u32[]{:S(2)}, u32[]{:S(2)}) collective-permute-start(bf16[16,5120]{1,0:T(8,128)(2,1)} %refs_0_.1), channel_id=1, source_target_pairs={{0,1},{1,0},{2,3},{3,2},{4,5},{5,4},{6,7},{7,6},{8,9},{9,8},{10,11... | collective-permute-start | bytes 491528 | tf_op jit(solution)/shard_map/ppermute | solution.py:39
  18.0 27.9 %collective-permute-start.19 = (bf16[128,256]{1,0:T(8,128)(2,1)}, bf16[128,256]{1,0:T(8,128)(2,1)S(1)}, u32[]{:S(2)}, u32[]{:S(2)}) collective-permute-start(bf16[128,256]{1,0:T(8,128)(2,1)} %get-tuple-element.65), channel_id=1, source_target_pairs={{0,16},{8,24},{16,0},{24,8},{32,48},{40,56},{48,32},{56,40},{64,80... | collective-permute-start | bytes 196616 | tf_op jit(solution)/shard_map/ppermute | solution.py:44
  21.2 20.3 %collective-permute-start.18 = (bf16[128,256]{1,0:T(8,128)(2,1)S(1)}, bf16[128,256]{1,0:T(8,128)(2,1)S(1)}, u32[]{:S(2)}, u32[]{:S(2)}) collective-permute-start(bf16[128,256]{1,0:T(8,128)(2,1)S(1)} %get-tuple-element.67), channel_id=1, source_target_pairs={{0,8},{8,16},{16,24},{24,0},{32,40},{40,48},{48,56},{56,32},{64,72... | collective-permute-start | bytes 196616 | tf_op jit(solution)/shard_map/ppermute | solution.py:44
  51.7 57.3 %collective-permute-start.27 = (bf16[1024,256]{1,0:T(8,128)(2,1)S(1)}, bf16[1024,256]{1,0:T(8,128)(2,1)}, u32[]{:S(2)}, u32[]{:S(2)}) collective-permute-start(bf16[1024,256]{1,0:T(8,128)(2,1)S(1)} %bitcast.62), channel_id=1, source_target_pairs={{0,8},{8,16},{16,24},{24,0},{32,40},{40,48},{48,56},{56,32},{64,72... | collective-permute-start | bytes 1572872 | tf_op jit(solution)/shard_map/ppermute | solution.py:44
  53.1 19.7 %collective-permute-start.23 = (bf16[2,128,256]{2,1,0:T(8,128)(2,1)S(1)}, bf16[2,128,256]{2,1,0:T(8,128)(2,1)S(1)}, u32[]{:S(2)}, u32[]{:S(2)}) collective-permute-start(bf16[2,128,256]{2,1,0:T(8,128)(2,1)S(1)} %pad_maximum_fusion.3.refs_8_), channel_id=1, source_target_pairs={{0,96},{8,104},{16,112},{24,120},{32,0},{40,8},{48,16},{56,24},{64... | collective-permute-start | bytes 393224 | tf_op jit(solution)/shard_map/ppermute | solution.py:44
  56.1 18.8 %collective-permute-start.24 = (bf16[2,128,256]{2,1,0:T(8,128)(2,1)S(1)}, bf16[2,128,256]{2,1,0:T(8,128)(2,1)S(1)}, u32[]{:S(2)}, u32[]{:S(2)}) collective-permute-start(bf16[2,128,256]{2,1,0:T(8,128)(2,1)S(1)} %pad_maximum_fusion.4.refs_9_), channel_id=1, source_target_pairs={{0,96},{8,104},{16,112},{24,120},{32,0},{40,8},{48,16},{56,24},{64... | collective-permute-start | bytes 393224 | tf_op jit(solution)/shard_map/ppermute | solution.py:44
  56.1 20.5 %collective-permute-start.22 = (bf16[2,128,256]{2,1,0:T(8,128)(2,1)S(1)}, bf16[2,128,256]{2,1,0:T(8,128)(2,1)S(1)}, u32[]{:S(2)}, u32[]{:S(2)}) collective-permute-start(bf16[2,128,256]{2,1,0:T(8,128)(2,1)S(1)} %pad_maximum_fusion.4.refs_9_), channel_id=1, source_target_pairs={{0,32},{8,40},{16,48},{24,56},{32,64},{40,72},{48,80},{56,88},{64,... | collective-permute-start | bytes 393224 | tf_op jit(solution)/shard_map/ppermute | solution.py:44
  58.1 19.7 %collective-permute-start.25 = (bf16[2,128,256]{2,1,0:T(8,128)(2,1)S(1)}, bf16[2,128,256]{2,1,0:T(8,128)(2,1)S(1)}, u32[]{:S(2)}, u32[]{:S(2)}) collective-permute-start(bf16[2,128,256]{2,1,0:T(8,128)(2,1)S(1)} %collective-permute-done.21.refs_10_), channel_id=1, source_target_pairs={{0,32},{8,40},{16,48},{24,56},{32,64},{40,72},{48,80},{56,88},{64,... | collective-permute-start | bytes 393224 | tf_op jit(solution)/shard_map/ppermute | solution.py:44
  72.8 36.6 %collective-permute-start.30 = (bf16[1024,256]{1,0:T(8,128)(2,1)S(1)}, bf16[1024,256]{1,0:T(8,128)(2,1)}, u32[]{:S(2)}, u32[]{:S(2)}) collective-permute-start(bf16[1024,256]{1,0:T(8,128)(2,1)S(1)} %bitcast.59), channel_id=1, source_target_pairs={{0,24},{8,0},{16,8},{24,16},{32,56},{40,32},{48,40},{56,48},{64,88... | collective-permute-start | bytes 1572872 | tf_op jit(solution)/shard_map/ppermute | solution.py:44
  76.6 38.6 %collective-permute-start.29 = (bf16[1024,256]{1,0:T(8,128)(2,1)S(1)}, bf16[1024,256]{1,0:T(8,128)(2,1)S(1)}, u32[]{:S(2)}, u32[]{:S(2)}) collective-permute-start(bf16[1024,256]{1,0:T(8,128)(2,1)S(1)} %bitcast.63), channel_id=1, source_target_pairs={{0,24},{8,0},{16,8},{24,16},{32,56},{40,32},{48,40},{56,48},{64,88... | collective-permute-start | bytes 1572872 | tf_op jit(solution)/shard_map/ppermute | solution.py:44
  77.8 37.4 %collective-permute-start.28 = (bf16[1024,256]{1,0:T(8,128)(2,1)S(1)}, bf16[1024,256]{1,0:T(8,128)(2,1)S(1)}, u32[]{:S(2)}, u32[]{:S(2)}) collective-permute-start(bf16[1024,256]{1,0:T(8,128)(2,1)S(1)} %bitcast.60), channel_id=1, source_target_pairs={{0,8},{8,16},{16,24},{24,0},{32,40},{40,48},{48,56},{56,32},{64,72... | collective-permute-start | bytes 1572872 | tf_op jit(solution)/shard_map/ppermute | solution.py:44
  81.5 19.0 %collective-permute-start.11 = (bf16[144,256]{1,0:T(8,128)(2,1)S(1)}, bf16[144,256]{1,0:T(8,128)(2,1)S(1)}, u32[]{:S(2)}, u32[]{:S(2)}) collective-permute-start(bf16[144,256]{1,0:T(8,128)(2,1)S(1)} %get-tuple-element.58), channel_id=1, source_target_pairs={{0,24},{8,0},{16,8},{24,16},{32,56},{40,32},{48,40},{56,48},{64,88... | collective-permute-start | bytes 221192 | tf_op jit(solution)/shard_map/ppermute | solution.py:44
  109.0 20.4 %collective-permute-start.31 = (bf16[1024,256]{1,0:T(8,128)(2,1)}, bf16[1024,256]{1,0:T(8,128)(2,1)}, u32[]{:S(2)}, u32[]{:S(2)}) collective-permute-start(bf16[1024,256]{1,0:T(8,128)(2,1)} %collective-permute-done.27.refs_18_), channel_id=1, source_target_pairs={{0,8},{8,16},{16,24},{24,0},{32,40},{40,48},{48,56},{56,32},{64,72... | collective-permute-start | bytes 1572872 | tf_op jit(solution)/shard_map/ppermute | solution.py:44
  109.4 20.0 %collective-permute-start.32 = (bf16[1024,256]{1,0:T(8,128)(2,1)}, bf16[1024,256]{1,0:T(8,128)(2,1)}, u32[]{:S(2)}, u32[]{:S(2)}) collective-permute-start(bf16[1024,256]{1,0:T(8,128)(2,1)} %collective-permute-done.30.refs_21_), channel_id=1, source_target_pairs={{0,24},{8,0},{16,8},{24,16},{32,56},{40,32},{48,40},{56,48},{64,88... | collective-permute-start | bytes 1572872 | tf_op jit(solution)/shard_map/ppermute | solution.py:44
  176.6 71.9 %reduce-scatter.3.cloned.1.call-start = ((), (), s32[]{:S(2)}) async-start(), calls=%async_computation.2 | async-start | bytes 1310720 | tf_op jit(solution)/shard_map/reduce_scatter | solution.py:443
  189.2 24.9 %collective-permute-start.47 = (bf16[1024,256]{1,0:T(8,128)(2,1)}, bf16[1024,256]{1,0:T(8,128)(2,1)}, u32[]{:S(2)}, u32[]{:S(2)}) collective-permute-start(bf16[1024,256]{1,0:T(8,128)(2,1)} %get-tuple-element.36), channel_id=1, source_target_pairs={{0,24},{8,0},{16,8},{24,16},{32,56},{40,32},{48,40},{56,48},{64,88... | collective-permute-start | bytes 1572872 | tf_op jit(solution)/shard_map/ppermute | solution.py:44
  191.7 28.7 %collective-permute-start.43 = (bf16[1024,256]{1,0:T(8,128)(2,1)}, bf16[1024,256]{1,0:T(8,128)(2,1)}, u32[]{:S(2)}, u32[]{:S(2)}) collective-permute-start(bf16[1024,256]{1,0:T(8,128)(2,1)} %get-tuple-element.31), channel_id=1, source_target_pairs={{0,8},{8,16},{16,24},{24,0},{32,40},{40,48},{48,56},{56,32},{64,72... | collective-permute-start | bytes 1572872 | tf_op jit(solution)/shard_map/ppermute | solution.py:44
  210.8 33.0 %collective-permute-start.45 = (bf16[1024,256]{1,0:T(8,128)(2,1)}, bf16[1024,256]{1,0:T(8,128)(2,1)}, u32[]{:S(2)}, u32[]{:S(2)}) collective-permute-start(bf16[1024,256]{1,0:T(8,128)(2,1)} %get-tuple-element.32), channel_id=1, source_target_pairs={{0,24},{8,0},{16,8},{24,16},{32,56},{40,32},{48,40},{56,48},{64,88... | collective-permute-start | bytes 1572872 | tf_op jit(solution)/shard_map/ppermute | solution.py:44
  214.0 32.4 %collective-permute-start.46 = (bf16[1024,256]{1,0:T(8,128)(2,1)}, bf16[1024,256]{1,0:T(8,128)(2,1)}, u32[]{:S(2)}, u32[]{:S(2)}) collective-permute-start(bf16[1024,256]{1,0:T(8,128)(2,1)} %get-tuple-element.34), channel_id=1, source_target_pairs={{0,8},{8,16},{16,24},{24,0},{32,40},{40,48},{48,56},{56,32},{64,72... | collective-permute-start | bytes 1572872 | tf_op jit(solution)/shard_map/ppermute | solution.py:44
  226.1 20.2 %collective-permute-start.48 = (bf16[1024,256]{1,0:T(8,128)(2,1)S(1)}, bf16[1024,256]{1,0:T(8,128)(2,1)S(1)}, u32[]{:S(2)}, u32[]{:S(2)}) collective-permute-start(bf16[1024,256]{1,0:T(8,128)(2,1)S(1)} %copy-done.28), channel_id=1, source_target_pairs={{0,24},{8,0},{16,8},{24,16},{32,56},{40,32},{48,40},{56,48},{64,88... | collective-permute-start | bytes 1572872 | tf_op jit(solution)/shard_map/ppermute | solution.py:44
  230.0 13.8 %collective-permute-start.44 = (bf16[1024,256]{1,0:T(8,128)(2,1)S(1)}, bf16[1024,256]{1,0:T(8,128)(2,1)S(1)}, u32[]{:S(2)}, u32[]{:S(2)}) collective-permute-start(bf16[1024,256]{1,0:T(8,128)(2,1)S(1)} %add_convert_fusion.3), channel_id=1, source_target_pairs={{0,8},{8,16},{16,24},{24,0},{32,40},{40,48},{48,56},{56,32},{64,72... | collective-permute-start | bytes 1572872 | tf_op jit(solution)/shard_map/ppermute | solution.py:44
  (72 other events, 910.2 us)
Sparse Core Ops, SparseCore 0:
  176.7 22.6 reduce-scatter.4
  214.2 22.7 reduce-scatter.2

commit v2 on v1

v2 whole, which is shorter than its diff:
```python
import functools
import math

import jax
import jax.numpy as jnp
from jax import lax
from jax.experimental import pallas as pl
from jax.experimental.pallas import tpu as pltpu
from jax.sharding import PartitionSpec as P

HD = 128
RESP_LEN = 32
ROWS = 128
SLICE = 256
STAT_ROWS = 16
CHUNK = 2048
HALF = 1024
PARTS = 5
KEYS = 8192
WROWS = 1024
BLOCK = 1024
SCALE = HD ** -0.5
EXP2_SCALE = SCALE * math.log2(math.e)
NEG = -1.0e30
BF = jnp.bfloat16
F32 = jnp.float32
NT = (((1,), (1,)), ((), ()))
NN = (((1,), (0,)), ((), ()))
TN = (((0,), (0,)), ((), ()))
ANY = pl.BlockSpec(memory_space=pl.ANY)
VM = pl.BlockSpec(memory_space=pltpu.VMEM)
SM = pl.BlockSpec(memory_space=pltpu.SMEM)
XG = [[a * 4 + b for a in range(4)] for b in range(4)]
YG = [[a * 4 + b for b in range(4)] for a in range(4)]


def dot(a, b, dims):
    return lax.dot_general(a, b, dims, preferred_element_type=F32)


def move_tp(x, dz, dc):
    pairs = [(z * 2 + c, ((z + dz) % 4) * 2 + (c + dc) % 2) for z in range(4) for c in range(2)]
    return lax.ppermute(x, "tp", pairs)


def move_seq(x, dx, dy):
    pairs = [(a * 4 + b, ((a + dx) % 4) * 4 + (b + dy) % 4) for a in range(4) for b in range(4)]
    return lax.ppermute(x, "seq", pairs)


def split3(v):
    hi = v.astype(BF).astype(F32)
    mid = (v - hi).astype(BF).astype(F32)
    return hi, mid, v - hi - mid


def stat_rows(first, second):
    rows = list(split3(first)) + list(split3(second))
    return jnp.concatenate(rows + [jnp.zeros((STAT_ROWS - 6, SLICE), F32)], axis=0).astype(BF)


def read_stats(rows):
    r = rows.astype(F32)
    return r[0:1] + r[1:2] + r[2:3], r[3:4] + r[4:5] + r[5:6]


def causal_mask(lens):
    key = lax.broadcasted_iota(jnp.int32, (ROWS, ROWS), 0)
    row = lax.broadcasted_iota(jnp.int32, (ROWS, ROWS), 1)
    member = lax.shift_right_logical(key, 5)
    length = jnp.where(member == 0, lens[0], jnp.where(member == 1, lens[1], jnp.where(member == 2, lens[2], lens[3])))
    live = (key & (RESP_LEN - 1)) < length
    return (member == lax.shift_right_logical(row, 5)) & (key <= row) & live


def wide_mask(meta):
    return jnp.concatenate([causal_mask([meta[4], meta[5], meta[6], meta[7]])] * 8, axis=1)


def stack(slices, into):
    for at in range(4):
        for j in range(2):
            n = (at * 2 + j) * HD
            into[n:n + HD] = slices[at, :ROWS, j * HD:(j + 1) * HD]


def stack_turned(y, slices, into):
    for n in range(4):
        for j in range(2):
            start = pl.multiple_of((((y + n) & 3) * 2 + j) * HD, HD)
            into[pl.ds(start, HD)] = slices[n][:ROWS, j * HD:(j + 1) * HD]


def live_rows(meta, shape):
    row = lax.broadcasted_iota(jnp.int32, shape, 0)
    member = lax.shift_right_logical(row, 5)
    length = jnp.where(member == 0, meta[4], jnp.where(member == 1, meta[5], jnp.where(member == 2, meta[6], meta[7])))
    return (row & (RESP_LEN - 1)) < length


def group_kernel(a, b, c, d, out):
    for n, piece in enumerate((a, b, c, d)):
        out[n * 16:(n + 1) * 16] = piece[...]


def group_rows(pieces):
    return pl.pallas_call(
        group_kernel,
        in_specs=[VM] * 4,
        out_specs=VM,
        out_shape=jax.ShapeDtypeStruct((64, pieces[0].shape[1]), BF),
        compiler_params=pltpu.CompilerParams(vmem_limit_bytes=6 << 20),
        name="group_rows",
    )(*pieces)


def near_kernel(*refs):
    ins, outs, sem = refs[:3], refs[-4:-1], refs[-1]
    copies = [pltpu.make_async_copy(src, dst, sem.at[n]) for n, (src, dst) in enumerate(zip(ins, outs))]
    for copy in copies:
        copy.start()
    for copy in copies:
        copy.wait()


def bring_near(weights, after=()):
    d = weights[0].shape[0]
    return pl.pallas_call(
        near_kernel,
        in_specs=[ANY] * (3 + len(after)),
        out_specs=[VM] * 3,
        out_shape=[pltpu.VMEM(w.shape, BF) for w in weights],
        scratch_shapes=[pltpu.SemaphoreType.DMA((3,))],
        compiler_params=pltpu.CompilerParams(vmem_limit_bytes=4 << 20),
        cost_estimate=pl.CostEstimate(flops=0, bytes_accessed=d * 2560, transcendentals=0),
        name="bring_near",
    )(*weights, *after)


def project_kernel(meta, *refs):
    pieces, (wq_s, wk_s, wv_s), cg = refs[:2], refs[2:5], refs[5]
    out, k_out, v_out, og = refs[6], refs[7], refs[8], refs[9:13]
    seg, q_all, og_all, sem = refs[13:]
    z, c = meta[2], meta[3]
    copies = []
    for rc in range(2):
        for dz in range(4):
            start = pl.multiple_of((((z - dz) & 3) * 2 + (c ^ rc)) * 16, 16)
            source = pieces[rc].at[pl.ds(dz * 16, 16)]
            copies.append(pltpu.make_async_copy(source, seg.at[pl.ds(start, 16)], sem.at[rc * 4 + dz]))
    for copy in copies:
        copy.start()
    live = live_rows(meta, (ROWS, SLICE))
    prompt = jnp.full((STAT_ROWS, SLICE), meta[8], jnp.int32).astype(F32).astype(BF)
    for n in range(4):
        start = pl.multiple_of(((meta[1] + n) & 3) * SLICE, SLICE)
        grads = cg[:, pl.ds(start, SLICE)]
        og[n][:ROWS] = jnp.where(live, grads, jnp.zeros_like(grads))
        og[n][ROWS:] = prompt
    stack_turned(meta[1], og, og_all)
    for copy in copies:
        copy.wait()
    k_out[...] = dot(seg[...], wk_s[...], NN).astype(BF)
    v_out[...] = dot(seg[...], wv_s[...], NN).astype(BF)
    q = dot(seg[...], wq_s[...], NN).astype(BF)
    for h in range(8):
        q_all[h * HD:(h + 1) * HD] = q[:, h * HD:(h + 1) * HD]
    mask = wide_mask(meta)
    s = jnp.where(mask, dot(k_out[...], q_all[...], NT) * SCALE, NEG)
    top = jnp.max(s, axis=0, keepdims=True)
    p = jnp.where(mask, jnp.exp(s - top), 0.0)
    total = jnp.sum(p, axis=0, keepdims=True)
    dp = dot(v_out[...], og_all[...], NT)
    lse = top + jnp.log(total)
    corr = jnp.sum(p.astype(BF).astype(F32) * dp, axis=0, keepdims=True) / total
    for at in range(4):
        cols = slice(at * SLICE, (at + 1) * SLICE)
        stats = stat_rows(lse[:, cols], corr[:, cols])
        out[at, :ROWS] = q[:, cols]
        out[at, ROWS:] = stats


def project(meta, pieces, wq, wk, wv, context_grad):
    d = wq.shape[0]
    return pl.pallas_call(
        project_kernel,
        in_specs=[SM] + [ANY] * 2 + [VM] * 4,
        out_specs=[VM] * 7,
        scratch_shapes=[
            pltpu.VMEM((ROWS, d), BF),
            pltpu.VMEM((WROWS, HD), BF),
            pltpu.VMEM((WROWS, HD), BF),
            pltpu.SemaphoreType.DMA((8,)),
        ],
        out_shape=[
            jax.ShapeDtypeStruct((4, ROWS + STAT_ROWS, SLICE), BF),
            jax.ShapeDtypeStruct((ROWS, HD), BF),
            jax.ShapeDtypeStruct((ROWS, HD), BF),
        ] + [jax.ShapeDtypeStruct((ROWS + STAT_ROWS, SLICE), BF)] * 4,
        compiler_params=pltpu.CompilerParams(vmem_limit_bytes=16 << 20),
        cost_estimate=pl.CostEstimate(flops=2 * ROWS * d * 1280, bytes_accessed=d * 1280 * 2, transcendentals=0),
        name="project",
    )(meta, *pieces, wq, wk, wv, context_grad)


def pack_kernel(q, g0, g1, g2, g3, out, h0, h1, h2, h3, sem):
    copies = [pltpu.make_async_copy(q, out.at[n], sem.at[n]) for n in range(4)]
    for copy in copies:
        copy.start()
    for src, dst in ((g0, h0), (g1, h1), (g2, h2), (g3, h3)):
        dst[...] = src[...]
    for copy in copies:
        copy.wait()


def pack(q, og):
    return pl.pallas_call(
        pack_kernel,
        in_specs=[VM] * 5,
        out_specs=[ANY] + [VM] * 4,
        out_shape=[jax.ShapeDtypeStruct((4,) + q.shape, BF)] + [jax.ShapeDtypeStruct(g.shape, BF) for g in og],
        scratch_shapes=[pltpu.SemaphoreType.DMA((4,))],
        compiler_params=pltpu.CompilerParams(vmem_limit_bytes=8 << 20),
        name="pack",
    )(q, *og)


def forward_kernel(sel, q_in, *refs):
    og_in, kv_in, refs = refs[:4], refs[4], refs[5:]
    ctx_out, q_all, og_all, scale_out, stat_out, p_hbm = refs[:6]
    qslot, ogslot, kv, p_all, s_even, s_odd, acc, mblk, m_ref, l_ref, sem_in, sem_kv, sem_out = refs[6:]
    blocks = KEYS // BLOCK

    kv_copies = kv_copies_of(kv_in, kv, sem_kv)
    copies, waits = [], []
    for r in range(4):
        copies.append(pltpu.make_async_copy(q_in.at[sel[r]], qslot.at[r], sem_in.at[r]))
        for n in range(4):
            @pl.when(sel[4 + r] == n)
            def _():
                pltpu.make_async_copy(og_in[n].at[sel[8 + r]], ogslot.at[r], sem_in.at[4 + r]).start()
        waits.append(pltpu.make_async_copy(og_in[0].at[0], ogslot.at[r], sem_in.at[4 + r]))
    for copy in copies:
        copy.start()
    for copy in kv_copies:
        copy.start()
    ctx_out[...] = jnp.zeros_like(ctx_out)
    m_ref[...] = jnp.full_like(m_ref, NEG)
    l_ref[...] = jnp.zeros_like(l_ref)
    acc[...] = jnp.zeros_like(acc)
    for copy in copies + waits:
        copy.wait()
    stack(qslot, q_all)
    stack(ogslot, og_all)

    def scores(b, into):
        keys = pl.ds(pl.multiple_of(b * BLOCK, BLOCK), BLOCK)
        into[...] = dot(kv[keys, :HD], q_all[...], NT)

    def soften(b, scored):
        keys = pl.ds(pl.multiple_of(b * BLOCK, BLOCK), BLOCK)
        s = scored[...]
        old = m_ref[...]
        new = jnp.maximum(old, jnp.max(s, axis=0, keepdims=True))
        p = jnp.exp2((s - new) * EXP2_SCALE)
        factor = jnp.exp2((old - new) * EXP2_SCALE)
        l_ref[...] = l_ref[...] * factor + jnp.sum(p, axis=0, keepdims=True)
        pb = p.astype(BF)
        p_all[keys, :] = pb
        pltpu.make_async_copy(p_all.at[keys], p_hbm.at[keys], sem_out.at[b]).start()
        acc[...] = acc[...] * factor + dot(kv[keys, HD:].T, pb, NN)
        m_ref[...] = new
        mblk[pl.ds(b, 1), :] = new

    kv_arrived(0, kv_in, kv, sem_kv)
    scores(0, s_even)

    def forward(b, _):
        kv_arrived(2 * b + 1, kv_in, kv, sem_kv)
        scores(2 * b + 1, s_odd)
        soften(2 * b, s_even)

        @pl.when(b < blocks // 2 - 1)
        def _():
            kv_arrived(2 * b + 2, kv_in, kv, sem_kv)
        scores(lax.rem(2 * b + 2, blocks), s_even)
        soften(2 * b + 1, s_odd)
        return 0

    lax.fori_loop(0, blocks // 2, forward, 0)

    for r in range(4):
        rs = slice(r * SLICE, (r + 1) * SLICE)
        lse0, corr0 = read_stats(qslot[r, ROWS:])
        lse = m_ref[:, rs] * SCALE + jnp.log(l_ref[:, rs])
        top = jnp.maximum(lse, lse0)
        log_norm = top + jnp.log(jnp.exp(lse - top) + jnp.exp(lse0 - top))
        inv = jnp.exp(lse - log_norm) / l_ref[:, rs]
        ctx = acc[:, rs] * inv
        ogt = og_all[rs].astype(F32).T
        corr = jnp.sum(ogt * ctx, axis=0, keepdims=True) + corr0 * jnp.exp(lse0 - log_norm)
        ctx_rows = ctx.T
        for j in range(2):
            ctx_out[sel[r], :, j * HD:(j + 1) * HD] = ctx_rows[j * HD:(j + 1) * HD].astype(BF)
        stat_out[0:1, rs] = log_norm
        stat_out[1:2, rs] = corr
        scale_out[:, rs] = jnp.exp2((mblk[:, rs] - m_ref[:, rs]) * EXP2_SCALE) * inv
    for b in range(blocks):
        keys = pl.ds(b * BLOCK, BLOCK)
        pltpu.make_async_copy(p_all.at[keys], p_hbm.at[keys], sem_out.at[b]).wait()


def kv_copies_of(kv_in, kv, sem):
    blocks = [pl.ds(n * BLOCK, BLOCK) for n in range(KEYS // BLOCK)]
    return [pltpu.make_async_copy(kv_in.at[rows], kv.at[rows], sem.at[n]) for n, rows in enumerate(blocks)]


def kv_arrived(b, kv_in, kv, sem):
    keys = pl.ds(pl.multiple_of(b * BLOCK, BLOCK), BLOCK)
    pltpu.make_async_copy(kv_in.at[keys], kv.at[keys], sem.at[b]).wait()


def backward_kernel(sel, q_all, og_all, factors, stats, p_hbm, *refs):
    kv_in, refs = refs[0], refs[1:]
    dq_out, dkv_out, kv, dkv, p_all, dqt, sem_kv, sem_p, sem_out = refs
    blocks = KEYS // BLOCK
    kv_copies = kv_copies_of(kv_in, kv, sem_kv)
    for b in range(blocks):
        keys = pl.ds(b * BLOCK, BLOCK)
        kv_copies[b].start()
        pltpu.make_async_copy(p_hbm.at[keys], p_all.at[keys], sem_p.at[b]).start()
    dq_out[...] = jnp.zeros_like(dq_out)
    dqt[...] = jnp.zeros_like(dqt)
    corr = stats[1:2]

    def backward(b, _):
        keys = pl.ds(pl.multiple_of(b * BLOCK, BLOCK), BLOCK)
        kv_arrived(b, kv_in, kv, sem_kv)
        dp = dot(kv[keys, HD:], og_all[...], NT)
        pltpu.make_async_copy(p_hbm.at[keys], p_all.at[keys], sem_p.at[b]).wait()
        a = p_all[keys, :].astype(F32) * factors[pl.ds(b, 1), :]
        ds = (a * (dp - corr)).astype(BF)
        dkv[keys, HD:] = dot(a.astype(BF), og_all[...], NN).astype(BF)
        dkv[keys, :HD] = (dot(ds, q_all[...], NN) * SCALE).astype(BF)
        pltpu.make_async_copy(dkv.at[keys], dkv_out.at[keys], sem_out.at[b]).start()
        dqt[...] += dot(kv[keys, :HD].T, ds, NN)
        return 0

    lax.fori_loop(0, blocks, backward, 0)
    for r in range(4):
        rs = slice(r * SLICE, (r + 1) * SLICE)
        rows = (dqt[:, rs] * SCALE).T
        for j in range(2):
            dq_out[sel[r], :ROWS, j * HD:(j + 1) * HD] = rows[j * HD:(j + 1) * HD].astype(BF)
        dq_out[sel[r], ROWS:] = stat_rows(stats[0:1, rs], stats[1:2, rs])
    for b in range(blocks):
        keys = pl.ds(b * BLOCK, BLOCK)
        pltpu.make_async_copy(dkv.at[keys], dkv_out.at[keys], sem_out.at[b]).wait()


def forward(sel, q_parts, og_parts, kv):
    blocks = KEYS // BLOCK
    return pl.pallas_call(
        forward_kernel,
        in_specs=[SM] + [ANY] * 6,
        out_specs=[VM] * 5 + [ANY],
        out_shape=[
            jax.ShapeDtypeStruct((16, ROWS, SLICE), BF),
            jax.ShapeDtypeStruct((WROWS, HD), BF),
            jax.ShapeDtypeStruct((WROWS, HD), BF),
            jax.ShapeDtypeStruct((blocks, WROWS), F32),
            jax.ShapeDtypeStruct((2, WROWS), F32),
            jax.ShapeDtypeStruct((KEYS, WROWS), BF),
        ],
        scratch_shapes=[
            pltpu.VMEM((4, ROWS + STAT_ROWS, SLICE), BF),
            pltpu.VMEM((4, ROWS + STAT_ROWS, SLICE), BF),
            pltpu.VMEM((KEYS, SLICE), BF),
            pltpu.VMEM((KEYS, WROWS), BF),
            pltpu.VMEM((BLOCK, WROWS), F32),
            pltpu.VMEM((BLOCK, WROWS), F32),
            pltpu.VMEM((HD, WROWS), F32),
            pltpu.VMEM((blocks, WROWS), F32),
            pltpu.VMEM((1, WROWS), F32),
            pltpu.VMEM((1, WROWS), F32),
            pltpu.SemaphoreType.DMA((8,)),
            pltpu.SemaphoreType.DMA((8,)),
            pltpu.SemaphoreType.DMA((blocks,)),
        ],
        compiler_params=pltpu.CompilerParams(vmem_limit_bytes=58 << 20),
        cost_estimate=pl.CostEstimate(flops=4 * WROWS * KEYS * HD, bytes_accessed=22 << 20, transcendentals=WROWS * KEYS),
        name="attention_forward",
    )(sel, q_parts, *og_parts, kv)


def backward(sel, q_all, og_all, factors, stats, p, kv):
    blocks = KEYS // BLOCK
    return pl.pallas_call(
        backward_kernel,
        in_specs=[SM] + [VM] * 4 + [ANY] * 2,
        out_specs=[VM, ANY],
        out_shape=[
            jax.ShapeDtypeStruct((16, ROWS + STAT_ROWS, SLICE), BF),
            jax.ShapeDtypeStruct((KEYS, SLICE), BF),
        ],
        scratch_shapes=[
            pltpu.VMEM((KEYS, SLICE), BF),
            pltpu.VMEM((KEYS, SLICE), BF),
            pltpu.VMEM((KEYS, WROWS), BF),
            pltpu.VMEM((HD, WROWS), F32),
            pltpu.SemaphoreType.DMA((8,)),
            pltpu.SemaphoreType.DMA((blocks,)),
            pltpu.SemaphoreType.DMA((blocks,)),
        ],
        compiler_params=pltpu.CompilerParams(vmem_limit_bytes=58 << 20),
        cost_estimate=pl.CostEstimate(flops=8 * WROWS * KEYS * HD, bytes_accessed=24 << 20, transcendentals=0),
        name="attention_backward",
    )(sel, q_all, og_all, factors, stats, p, kv)


def hidden_kernel(meta, dq_in, qs, og0, og1, og2, og3, k, v, wq, wk, wv, out, q_all, og_all, dq_got, dq_s, dk_s, dv_s, part, sem):
    fetch = pltpu.make_async_copy(dq_in.at[meta[8]], dq_got, sem.at[0])
    fetch.start()
    size = part.shape[1]
    stack(qs, q_all)
    stack_turned(meta[1], (og0, og1, og2, og3), og_all)
    mask = wide_mask(meta)
    s = dot(k[...], q_all[...], NT) * SCALE
    dp = dot(v[...], og_all[...], NT)
    fetch.wait()
    stats = [read_stats(dq_got[at, ROWS:]) for at in range(4)]
    log_norm = jnp.concatenate([t[0] for t in stats], axis=1)
    corr = jnp.concatenate([t[1] for t in stats], axis=1)
    a = jnp.where(mask, jnp.exp(jnp.where(mask, s - log_norm, 0.0)), 0.0)
    ds = (a * (dp - corr)).astype(BF)
    dk_s[...] = (dot(ds, q_all[...], NN) * SCALE).astype(BF)
    dv_s[...] = dot(a.astype(BF), og_all[...], NN).astype(BF)
    for h in range(8):
        cols = slice(h % 2 * HD, (h % 2 + 1) * HD)
        own = dot(ds[:, h * HD:(h + 1) * HD], k[...], TN) * SCALE
        dq_s[:, h * HD:(h + 1) * HD] = (dq_got[h // 2, :ROWS, cols].astype(F32) + own).astype(BF)

    z, c = meta[2], meta[3]
    for n in range(PARTS):
        at = slice(n * size, (n + 1) * size)
        part[...] = dot(dq_s[...], wq[at], NT) + dot(dk_s[...], wk[at], NT) + dot(dv_s[...], wv[at], NT)
        for rc in range(2):
            for dz in range(4):
                start = pl.multiple_of((((z + dz) & 3) * 2 + (c ^ rc)) * 16, 16)
                out[rc, dz, :, at] = part[pl.ds(start, 16), :].astype(BF)


def hidden_grad_parts(meta, dq, q, og, k, v, wq, wk, wv):
    d = wq.shape[0]
    return pl.pallas_call(
        hidden_kernel,
        in_specs=[SM, ANY] + [VM] * 10,
        out_specs=VM,
        scratch_shapes=[
            pltpu.VMEM((WROWS, HD), BF),
            pltpu.VMEM((WROWS, HD), BF),
            pltpu.VMEM((4, ROWS + STAT_ROWS, SLICE), BF),
            pltpu.VMEM((ROWS, 1024), BF),
            pltpu.VMEM((ROWS, HD), BF),
            pltpu.VMEM((ROWS, HD), BF),
            pltpu.VMEM((ROWS, d // PARTS), F32),
            pltpu.SemaphoreType.DMA((1,)),
        ],
        out_shape=jax.ShapeDtypeStruct((2, 4, 16, d), BF),
        compiler_params=pltpu.CompilerParams(vmem_limit_bytes=16 << 20),
        cost_estimate=pl.CostEstimate(flops=2 * ROWS * d * 1280, bytes_accessed=d * 1280 * 2, transcendentals=0),
        name="hidden_grad",
    )(meta, dq, q, *og, k, v, wq, wk, wv)


def context_kernel(meta, ctx, q, k, v, dq, after, out, q_all):
    stack(q, q_all)
    log_norm = jnp.concatenate([read_stats(dq[0, at, ROWS:])[0] for at in range(4)], axis=1)
    mask = wide_mask(meta)
    live = live_rows(meta, (ROWS, HD))
    s = dot(k[...], q_all[...], NT) * SCALE
    a = jnp.where(mask, jnp.exp(jnp.where(mask, s - log_norm, 0.0)), 0.0).astype(BF)
    for h in range(8):
        cols = slice(h % 2 * HD, (h % 2 + 1) * HD)
        own = dot(a[:, h * HD:(h + 1) * HD], v[...], TN)
        out[:, h * HD:(h + 1) * HD] = jnp.where(live, ctx[h // 2, :, cols].astype(F32) + own, 0.0).astype(BF)


def finish_context(meta, ctx, q, k, v, dq, after):
    rows = ROWS + STAT_ROWS
    return pl.pallas_call(
        context_kernel,
        grid_spec=pltpu.PrefetchScalarGridSpec(
            num_scalar_prefetch=1,
            grid=(1,),
            in_specs=[
                pl.BlockSpec((4, ROWS, SLICE), lambda i, m: (0, 0, 0)),
                pl.BlockSpec((4, rows, SLICE), lambda i, m: (0, 0, 0)),
                pl.BlockSpec((ROWS, HD), lambda i, m: (0, 0)),
                pl.BlockSpec((ROWS, HD), lambda i, m: (0, 0)),
                pl.BlockSpec((1, 4, rows, SLICE), lambda i, m: (m[8], 0, 0, 0)),
                ANY,
            ],
            out_specs=pl.BlockSpec((ROWS, 1024), lambda i, m: (0, 0)),
            scratch_shapes=[pltpu.VMEM((WROWS, HD), BF)],
        ),
        out_shape=jax.ShapeDtypeStruct((ROWS, 1024), BF),
        compiler_params=pltpu.CompilerParams(vmem_limit_bytes=16 << 20),
        name="context",
    )(meta, ctx, q, k, v, dq, after)


def exchange(parts):
    return lax.all_to_all(parts.reshape(16, -1, SLICE), "seq", 0, 0, tiled=True)


def add(*terms):
    return sum(t.astype(F32) for t in terms).astype(BF)


def on_device(hidden, wq, wk, wv, prefix_cache, owner_prompt, response_length, context_grad):
    seq, tp = lax.axis_index("seq"), lax.axis_index("tp")
    x, y, z, c = seq // 4, seq % 4, tp // 2, tp % 2
    place = jnp.stack([x, y, z, c]).astype(jnp.int32)
    meta = jnp.concatenate([place, response_length, owner_prompt])

    kv = lax.all_gather(prefix_cache.reshape(CHUNK, SLICE), "seq", axis=0, tiled=True, axis_index_groups=YG)

    passed = [move_tp(hidden, n, 0) for n in (1, 2, 3)]
    group = group_rows([hidden] + passed)
    near = bring_near((wq, wk, wv), (group,))
    q, k, v, *og = project(meta, [group, move_tp(group, 0, 1)], *near, context_grad)
    packed, *og = pack(q, og)
    q_parts = exchange(packed)
    og_row = jnp.stack([og[0]] + [move_seq(og[n], 0, n) for n in (1, 2, 3)])
    og_parts = [og_row] + [move_seq(og_row, n, 0) for n in (1, 2, 3)]

    prompts = jnp.concatenate([part[:, ROWS, 0] for part in og_parts]).astype(jnp.int32)
    owners = jnp.arange(16, dtype=jnp.int32)
    match = prompts == x
    owner = (x - owners // 4) % 4 * 4 + (y - owners) % 4
    rank = jnp.sum(match[None, :] & (owners[None, :] < owners[:, None]), axis=1)
    chosen = match[None, :] & (rank[None, :] == jnp.arange(4)[:, None])
    sel = jnp.sum(jnp.where(chosen, owner[None, :], 0), axis=1)
    spot = jnp.sum(jnp.where(chosen, owners[None, :], 0), axis=1)
    sel = jnp.concatenate([sel, spot // 4, spot % 4]).astype(jnp.int32)

    ctx_dense, q_all, og_all, factors, stats, weights = forward(sel, q_parts, og_parts, kv)
    ctx_row = lax.psum_scatter(ctx_dense.reshape(-1, SLICE), "seq", scatter_dimension=0, tiled=True, axis_index_groups=XG)
    dq_dense, dkv = backward(sel, q_all, og_all, factors, stats, weights, kv)
    dq = exchange(dq_dense).reshape(4, 4, ROWS + STAT_ROWS, SLICE)
    prefix_grad = lax.psum_scatter(dkv, "seq", scatter_dimension=0, tiled=True, axis_index_groups=YG)
    prefix_grad = prefix_grad.reshape(CHUNK, 1, 2, HD)

    parts = hidden_grad_parts(meta, dq, q, og, k, v, wq, wk, wv)
    pair = add(parts[0], move_tp(parts[1], 0, 1))
    hidden_grad = add(pair[0], *[move_tp(pair[n], n, 0) for n in (1, 2, 3)])

    ctx_parts = lax.all_to_all(ctx_row.reshape(4, ROWS, SLICE), "seq", 0, 0, tiled=True, axis_index_groups=YG)
    context = finish_context(meta, ctx_parts, q, k, v, dq, parts)
    return context, hidden_grad, prefix_grad


def solution(mesh):
    return jax.shard_map(
        on_device,
        mesh=mesh,
        in_specs=(
            P(("seq", "tp"), None),
            P(None, "tp"),
            P(None, "tp"),
            P(None, "tp"),
            P("seq", "tp", None, None),
            P("seq"),
            P("seq"),
            P("seq", "tp"),
        ),
        out_specs=(P("seq", "tp"), P(("seq", "tp"), None), P("seq", "tp", None, None)),
        check_vma=False,
    )
```

time: 277 us -> 190 us (0.69)
  starting transfers between devices: 74.5 us -> 33.2 us
  Pallas kernels: 92.4 us -> 54.5 us
  local copies, waits for them, and re-layouts: 35.5 us -> 18.9 us
  waiting for transfers between devices: 30.5 us -> 42.5 us
  other arithmetic: 11.1 us -> 2.95 us
  blocking collectives: 15.3 us -> 22.2 us
    ppermute x36 -> x6, starting transfers between devices: 62.9 us -> 11.5 us  [move_seq(): return lax.ppermute(x, 'seq', pairs)]
    pallas_call x9 -> x8, Pallas kernels: 92.4 us -> 54.5 us  [the longest x1 22 us: backward(): pl.pallas_call(backward_kernel, in_specs=[SM] + [VM] * 4 + [ANY] * 2, out...]
    all_to_all x0 -> x1, blocking collectives: none -> 22.2 us  [exchange(): return lax.all_to_all(parts.reshape(16, -1, SLICE), 'seq', 0, 0, tiled=True)]
    unnamed x1 -> x0, blocking collectives: 15.3 us -> none
    unnamed x95 -> x33, local copies, waits for them, and re-layouts: 25.4 us -> 15.4 us
    all_to_all x0 -> x2, starting transfers between devices: none -> 9.68 us  [the longest x1 6.28 us: exchange(): return lax.all_to_all(parts.reshape(16, -1, SLICE), 'seq', 0, 0, tiled=True)]
    convert_element_type x6 -> x2, other arithmetic: 10.6 us -> 1.91 us  [add(): return sum((t.astype(F32) for t in terms)).astype(BF)]
    ppermute x13 -> x8, waiting for transfers between devices: 5.17 us -> 11.8 us  [move_tp(): return lax.ppermute(x, 'tp', pairs)]
  transfers between devices with their start and end apart: 51 -> 19, of which waited for: 9 -> 12; matrix products, arithmetic and copies ran while one was open for 9% -> 2% of each run, Pallas kernels for 16% -> 19%
where the time goes in v2:
time: 190 us; the launch traced here: 189 us
  Pallas kernels  54.5 us (29%)
  waiting for transfers between devices  42.5 us (22%)
  starting transfers between devices  33.2 us (17%)
  blocking collectives  22.2 us (12%)
  local copies, waits for them, and re-layouts  18.9 us (10%)
  between operations  14.7 us (8%)
  other arithmetic  2.95 us (2%)
    ppermute x6, waiting for transfers between devices, move_seq(): return lax.ppermute(x, 'seq', pairs)  25.5 us
    all_to_all x1, blocking collectives, exchange(): return lax.all_to_all(parts.reshape(16, -1, SLICE), 'seq', 0, 0, tiled=True)  22.2 us
    pallas_call x1, Pallas kernels, backward(): pl.pallas_call(backward_kernel, in_specs=[SM] + [VM] * 4 + [ANY] * 2, out...  22 us
    pallas_call x1, Pallas kernels, forward(): pl.pallas_call(forward_kernel, in_specs=[SM] + [ANY] * 6, out_specs=[VM]...  18 us
    unnamed x33, local copies, waits for them, and re-layouts  15.4 us
    ppermute x8, waiting for transfers between devices, move_tp(): return lax.ppermute(x, 'tp', pairs)  11.8 us
    ppermute x8, starting transfers between devices, move_tp(): return lax.ppermute(x, 'tp', pairs)  11.7 us
    ppermute x6, starting transfers between devices, move_seq(): return lax.ppermute(x, 'seq', pairs)  11.5 us
  transfers between devices with their start and end apart: 19, of which 12 were waited for; matrix products, arithmetic and copies ran while one was open for 2% of the time, Pallas kernels for 19%

profile of v2, /device:TPU:0, one launch (start us, length us, event | category | flops | bytes accessed | tf_op | source)
XLA Modules:
  0.0 188.9 jit_solution(7370993384133136146)
XLA Ops:
  7.2 2.4 %copy.16 = bf16[256,8,2,128]{3,1,2,0:T(8,128)(2,1)} copy(bf16[256,8,2,128]{3,2,1,0:T(2,128)(2,1)} %bitcast.40) | data formatting | bytes 2097152
  9.7 4.0 %collective-permute-start.1 = (bf16[16,5120]{1,0:T(8,128)(2,1)S(1)}, bf16[16,5120]{1,0:T(8,128)(2,1)S(1)}, u32[]{:S(2)}, u32[]{:S(2)}) collective-permute-start(bf16[16,5120]{1,0:T(8,128)(2,1)S(1)} %copy-done.7), channel_id=1, source_target_pairs={{0,4},{1,5},{2,6},{3,7},{4,0},{5,1},{6,2},{7,3},{8,12},{9,13},{10,... | collective-permute-start | bytes 491528 | tf_op jit(solution)/shard_map/ppermute | solution.py:43
  14.8 2.2 %collective-permute-start.2 = (bf16[16,5120]{1,0:T(8,128)(2,1)S(1)}, bf16[16,5120]{1,0:T(8,128)(2,1)S(1)}, u32[]{:S(2)}, u32[]{:S(2)}) collective-permute-start(bf16[16,5120]{1,0:T(8,128)(2,1)S(1)} %copy-done.7), channel_id=1, source_target_pairs={{0,6},{1,7},{2,0},{3,1},{4,2},{5,3},{6,4},{7,5},{8,14},{9,15},{10,... | collective-permute-start | bytes 491528 | tf_op jit(solution)/shard_map/ppermute | solution.py:43
  18.8 2.7 %collective-permute-done.b = bf16[16,5120]{1,0:T(8,128)(2,1)S(1)} collective-permute-done((bf16[16,5120]{1,0:T(8,128)(2,1)S(1)}, bf16[16,5120]{1,0:T(8,128)(2,1)S(1)}, u32[]{:S(2)}, u32[]{:S(2)}) %collective-permute-start) | collective-permute-done | bytes 163872 | tf_op jit(solution)/shard_map/ppermute | solution.py:43
  23.1 4.4 %copy-done = bf16[5120,1024]{1,0:T(8,128)(2,1)S(1)} copy-done((bf16[5120,1024]{1,0:T(8,128)(2,1)S(1)}, bf16[5120,1024]{1,0:T(8,128)(2,1)}, u32[]{:S(2)}) %copy-start) | copy-done | bytes 10485784
  28.4 5.2 %project.1 = (bf16[4,144,256]{2,1,0:T(8,128)(2,1)S(1)}, bf16[128,128]{1,0:T(8,128)(2,1)S(1)}, bf16[128,128]{1,0:T(8,128)(2,1)S(1)}, bf16[144,256]{1,0:T(8,128)(2...) custom-call(s32[9]{0:T(128)S(1)} %concatenate.21.meta, ...), custom_call_target="tpu_custom_call" | custom-call | flops 1677721600 | bytes 13107200 | tf_op jit(solution)/shard_map/project/pallas_call | solution.py:185
  36.4 2.9 %collective-permute-start.5 = (bf16[144,256]{1,0:T(8,128)(2,1)S(1)}, bf16[144,256]{1,0:T(8,128)(2,1)S(1)}, u32[]{:S(2)}, u32[]{:S(2)}) collective-permute-start(bf16[144,256]{1,0:T(8,128)(2,1)S(1)} %get-tuple-element.36.og2), channel_id=1, source_target_pairs={{0,16},{8,24},{16,0},{24,8},{32,48},{40,56},{48,32},{56,40},{64,80... | collective-permute-start | bytes 221192 | tf_op jit(solution)/shard_map/ppermute | solution.py:48
  42.5 4.4 %collective-permute-done.5 = bf16[144,256]{1,0:T(8,128)(2,1)S(1)} collective-permute-done((bf16[144,256]{1,0:T(8,128)(2,1)S(1)}, bf16[144,256]{1,0:T(8,128)(2,1)S(1)}, u32[]{:S(2)}, u32[]{:S(2)}) %collective-permute-start.5) | collective-permute-done | bytes 73760 | tf_op jit(solution)/shard_map/ppermute | solution.py:48
  46.9 2.8 %collective-permute-start.9 = (bf16[4,144,256]{2,1,0:T(8,128)(2,1)S(1)}, bf16[4,144,256]{2,1,0:T(8,128)(2,1)S(1)}, u32[]{:S(2)}, u32[]{:S(2)}) collective-permute-start(bf16[4,144,256]{2,1,0:T(8,128)(2,1)S(1)} %pad_maximum_fusion.refs_0_), channel_id=1, source_target_pairs={{0,96},{8,104},{16,112},{24,120},{32,0},{40,8},{48,16},{56,24},{64... | collective-permute-start | bytes 884744 | tf_op jit(solution)/shard_map/ppermute | solution.py:48
  50.5 6.3 %all-to-all-start = ((bf16[16,144,256]{2,1,0:T(8,128)(2,1)}), bf16[16,144,256]{2,1,0:T(8,128)(2,1)S(1)}, u32[]{:S(2)}, u32[]{:S(2)}) async-start(bf16[16,144,256]{2,1,0:T(8,128)(2,1)} %bitcast.8), calls=%async_computation | async-start | bytes 2359296 | tf_op jit(solution)/shard_map/all_to_all | solution.py:514
  56.9 2.0 %collective-permute-start.7 = (bf16[4,144,256]{2,1,0:T(8,128)(2,1)S(1)}, bf16[4,144,256]{2,1,0:T(8,128)(2,1)S(1)}, u32[]{:S(2)}, u32[]{:S(2)}) collective-permute-start(bf16[4,144,256]{2,1,0:T(8,128)(2,1)S(1)} %pad_maximum_fusion.refs_0_), channel_id=1, source_target_pairs={{0,32},{8,40},{16,48},{24,56},{32,64},{40,72},{48,80},{56,88},{64,... | collective-permute-start | bytes 884744 | tf_op jit(solution)/shard_map/ppermute | solution.py:48
  59.0 7.6 %collective-permute-done.9.refs_3_ = bf16[4,144,256]{2,1,0:T(8,128)(2,1)S(1)} collective-permute-done((bf16[4,144,256]{2,1,0:T(8,128)(2,1)S(1)}, bf16[4,144,256]{2,1,0:T(8,128)(2,1)S(1)}, u32[]{:S(2)}, u32[]{:S(2)}) %collective-permute-start.9) | collective-permute-done | bytes 294944 | tf_op jit(solution)/shard_map/ppermute | solution.py:48
  66.9 11.6 %collective-permute-done.7.refs_1_ = bf16[4,144,256]{2,1,0:T(8,128)(2,1)S(1)} collective-permute-done((bf16[4,144,256]{2,1,0:T(8,128)(2,1)S(1)}, bf16[4,144,256]{2,1,0:T(8,128)(2,1)S(1)}, u32[]{:S(2)}, u32[]{:S(2)}) %collective-permute-start.7) | collective-permute-done | bytes 294944 | tf_op jit(solution)/shard_map/ppermute | solution.py:48
  80.6 18.0 %attention_forward.1 = (bf16[16,128,256]{2,1,0:T(8,128)(2,1)}, bf16[1024,128]{1,0:T(8,128)(2,1)}, bf16[1024,128]{1,0:T(8,128)(2,1)}, f32[8,1024]{1,0:T(8,128)}, ...) custom-call(s32[12]{0:T(128)} %pad_add_fusion.sel, bf16[16,144,256]{2,1,0:T(8,128)(2,1)} %copy-done.9, ...), custom_call_target="tpu_custom_call" | custom-call | flops 4294967296 | bytes 23068672 | tf_op jit(solution)/shard_map/attention_forward/pallas_call | solution.py:363
  98.9 22.0 %attention_backward.1 = (bf16[16,144,256]{2,1,0:T(8,128)(2,1)}, bf16[8192,256]{1,0:T(8,128)(2,1)}) custom-call(s32[12]{0:T(128)} %pad_add_fusion.sel, bf16[1024,128]{1,0:T(8,128)(2,1)} %get-tuple-element.42.q_all, bf16[1024,128]{1,0:T(8,128)(2,1)} %get-tuple-element.43.og_all, f32[8,1024]{1,0:T(8,128)} %get-tuple-element.44.factors, ...), custom_call_target="tpu_custom_call" | custom-call | flops 8589934592 | bytes 25165824 | tf_op jit(solution)/shard_map/attention_backward/pallas_call | solution.py:398
  122.1 22.2 %all_to_all.15 = bf16[16,144,256]{2,1,0:T(8,128)(2,1)S(1)} all-to-all(bf16[16,144,256]{2,1,0:T(8,128)(2,1)S(1)} %copy-done.10), channel_id=1, replica_groups=mesh['seq'=16,'tp'=8] {'seq'}, dimensions={0} | all-to-all | bytes 2359296 | tf_op jit(solution)/shard_map/all_to_all | solution.py:514
  144.3 4.1 %copy-done.1 = bf16[5120,1024]{1,0:T(8,128)(2,1)S(1)} copy-done((bf16[5120,1024]{1,0:T(8,128)(2,1)S(1)}, bf16[5120,1024]{1,0:T(8,128)(2,1)}, u32[]{:S(2)}) %copy-start.1) | copy-done | bytes 10485784
  149.7 5.6 %hidden_grad.1.after = bf16[2,4,16,5120]{3,2,1,0:T(8,128)(2,1)S(1)} custom-call(s32[9]{0:T(128)S(1)} %concatenate.21.meta, bf16[4,4,144,256]{3,2,1,0:T(8,128)(2,1)S(1)} %bitcast.36, bf16[4,144,256]{2,1,0:T(8,128)(2,1)S(1)} %get-tuple-element.29.q.qs, bf16[144,256]{1,0:T(8,128)(2,1)S(1)} %get-tuple-element.34.og0, ...), custom_call_target="tpu_custom_call" | custom-call | flops 1677721600 | bytes 13107200 | tf_op jit(solution)/shard_map/hidden_grad/pallas_call | solution.py:455
  155.5 2.1 %collective-permute-done.10 = bf16[4,16,5120]{2,1,0:T(8,128)(2,1)S(1)} collective-permute-done((bf16[4,16,5120]{2,1,0:T(8,128)(2,1)S(1)}, bf16[4,16,5120]{2,1,0:T(8,128)(2,1)S(1)}, u32[]{:S(2)}, u32[]{:S(2)}) %collective-permute-start.10) | collective-permute-done | bytes 655392 | tf_op jit(solution)/shard_map/ppermute | solution.py:43
  160.5 2.1 %collective-permute-start.13 = (bf16[16,5120]{1,0:T(8,128)(2,1)}, bf16[16,5120]{1,0:T(8,128)(2,1)S(1)}, u32[]{:S(2)}, u32[]{:S(2)}) collective-permute-start(bf16[16,5120]{1,0:T(8,128)(2,1)} %get-tuple-element.61), channel_id=1, source_target_pairs={{0,6},{1,7},{2,0},{3,1},{4,2},{5,3},{6,4},{7,5},{8,14},{9,15},{10,... | collective-permute-start | bytes 491528 | tf_op jit(solution)/shard_map/ppermute | solution.py:43
  163.6 3.4 %all-to-all-start.1 = ((bf16[4,128,256]{2,1,0:T(8,128)(2,1)}), bf16[4,128,256]{2,1,0:T(8,128)(2,1)S(1)}, u32[]{:S(2)}, u32[]{:S(2)}) async-start(bf16[4,128,256]{2,1,0:T(8,128)(2,1)} %bitcast.43), calls=%async_computation.2 | async-start | bytes 524288 | tf_op jit(solution)/shard_map/all_to_all | solution.py:559
  167.0 2.9 %collective-permute-done.13 = bf16[16,5120]{1,0:T(8,128)(2,1)S(1)} collective-permute-done((bf16[16,5120]{1,0:T(8,128)(2,1)}, bf16[16,5120]{1,0:T(8,128)(2,1)S(1)}, u32[]{:S(2)}, u32[]{:S(2)}) %collective-permute-start.13) | collective-permute-done | bytes 163872 | tf_op jit(solution)/shard_map/ppermute | solution.py:43
  173.3 4.2 %all-to-all-done.1.ctx = bf16[4,128,256]{2,1,0:T(8,128)(2,1)S(1)} async-done(((bf16[4,128,256]{2,1,0:T(8,128)(2,1)}), bf16[4,128,256]{2,1,0:T(8,128)(2,1)S(1)}, u32[]{:S(2)}, u32[]{:S(2)}) %all-to-all-start.1) | async-done | bytes 262176 | tf_op jit(solution)/shard_map/all_to_all | solution.py:559
  180.2 2.1 %reshape.108 = bf16[2048,1,2,128]{3,2,0,1:T(2,128)(2,1)} reshape(bf16[2048,256]{1,0:T(8,128)(2,1)} %reduce-scatter.5.cloned.1.call-done) | data formatting | bytes 2097152 | tf_op jit(solution)/shard_map/reshape | solution.py:553
  (76 shorter events, 27.1 us)
Async XLA Ops:
  7.2 72.4 %all-gather.2.cloned.1.call-start = ((), (), s32[]{:S(2)}) async-start(), calls=%async_computation.5 | async-start | bytes 5242880 | tf_op jit(solution)/shard_map/all_gather | solution.py:527
  7.2 15.9 %copy-start.4 = (bf16[5120,128]{1,0:T(8,128)(2,1)S(1)}, bf16[5120,128]{1,0:T(8,128)(2,1)}, u32[]{:S(2)}) copy-start(bf16[5120,128]{1,0:T(8,128)(2,1)} %wv.1) | copy-start | bytes 3932164
  9.7 13.4 %copy-start.12 = (s32[4]{0:T(128)S(1)}, s32[4]{0:T(128)}, u32[]{:S(2)}) copy-start(s32[4]{0:T(128)} %param.14) | copy-start | bytes 52
  9.7 13.4 %copy-start.2 = (bf16[5120,128]{1,0:T(8,128)(2,1)S(1)}, bf16[5120,128]{1,0:T(8,128)(2,1)}, u32[]{:S(2)}) copy-start(bf16[5120,128]{1,0:T(8,128)(2,1)} %wk.1) | copy-start | bytes 3932164
  9.7 9.1 %collective-permute-start.1 = (bf16[16,5120]{1,0:T(8,128)(2,1)S(1)}, bf16[16,5120]{1,0:T(8,128)(2,1)S(1)}, u32[]{:S(2)}, u32[]{:S(2)}) collective-permute-start(bf16[16,5120]{1,0:T(8,128)(2,1)S(1)} %copy-done.7), channel_id=1, source_target_pairs={{0,4},{1,5},{2,6},{3,7},{4,0},{5,1},{6,2},{7,3},{8,12},{9,13},{10,... | collective-permute-start | bytes 491528 | tf_op jit(solution)/shard_map/ppermute | solution.py:43
  13.8 7.7 %collective-permute-start = (bf16[16,5120]{1,0:T(8,128)(2,1)S(1)}, bf16[16,5120]{1,0:T(8,128)(2,1)S(1)}, u32[]{:S(2)}, u32[]{:S(2)}) collective-permute-start(bf16[16,5120]{1,0:T(8,128)(2,1)S(1)} %copy-done.7), channel_id=1, source_target_pairs={{0,2},{1,3},{2,4},{3,5},{4,6},{5,7},{6,0},{7,1},{8,10},{9,11},{10,... | collective-permute-start | bytes 491528 | tf_op jit(solution)/shard_map/ppermute | solution.py:43
  14.8 7.4 %collective-permute-start.2 = (bf16[16,5120]{1,0:T(8,128)(2,1)S(1)}, bf16[16,5120]{1,0:T(8,128)(2,1)S(1)}, u32[]{:S(2)}, u32[]{:S(2)}) collective-permute-start(bf16[16,5120]{1,0:T(8,128)(2,1)S(1)} %copy-done.7), channel_id=1, source_target_pairs={{0,6},{1,7},{2,0},{3,1},{4,2},{5,3},{6,4},{7,5},{8,14},{9,15},{10,... | collective-permute-start | bytes 491528 | tf_op jit(solution)/shard_map/ppermute | solution.py:43
  22.2 6.2 %collective-permute-start.3 = (bf16[64,5120]{1,0:T(8,128)(2,1)S(1)}, bf16[64,5120]{1,0:T(8,128)(2,1)}, u32[]{:S(2)}, u32[]{:S(2)}) collective-permute-start(bf16[64,5120]{1,0:T(8,128)(2,1)S(1)} %group_rows.1.refs_3_.refs_0_), channel_id=1, source_target_pairs={{0,1},{1,0},{2,3},{3,2},{4,5},{5,4},{6,7},{7,6},{8,9},{9,8},{10,11... | collective-permute-start | bytes 1966088 | tf_op jit(solution)/shard_map/ppermute | solution.py:43
  34.7 7.8 %collective-permute-start.4 = (bf16[144,256]{1,0:T(8,128)(2,1)S(1)}, bf16[144,256]{1,0:T(8,128)(2,1)S(1)}, u32[]{:S(2)}, u32[]{:S(2)}) collective-permute-start(bf16[144,256]{1,0:T(8,128)(2,1)S(1)} %get-tuple-element.35.og1), channel_id=1, source_target_pairs={{0,8},{8,16},{16,24},{24,0},{32,40},{40,48},{48,56},{56,32},{64,72... | collective-permute-start | bytes 221192 | tf_op jit(solution)/shard_map/ppermute | solution.py:48
  36.4 10.5 %collective-permute-start.5 = (bf16[144,256]{1,0:T(8,128)(2,1)S(1)}, bf16[144,256]{1,0:T(8,128)(2,1)S(1)}, u32[]{:S(2)}, u32[]{:S(2)}) collective-permute-start(bf16[144,256]{1,0:T(8,128)(2,1)S(1)} %get-tuple-element.36.og2), channel_id=1, source_target_pairs={{0,16},{8,24},{16,0},{24,8},{32,48},{40,56},{48,32},{56,40},{64,80... | collective-permute-start | bytes 221192 | tf_op jit(solution)/shard_map/ppermute | solution.py:48
  39.2 7.7 %collective-permute-start.6 = (bf16[144,256]{1,0:T(8,128)(2,1)S(1)}, bf16[144,256]{1,0:T(8,128)(2,1)S(1)}, u32[]{:S(2)}, u32[]{:S(2)}) collective-permute-start(bf16[144,256]{1,0:T(8,128)(2,1)S(1)} %get-tuple-element.37.og3), channel_id=1, source_target_pairs={{0,24},{8,0},{16,8},{24,16},{32,56},{40,32},{48,40},{56,48},{64,88... | collective-permute-start | bytes 221192 | tf_op jit(solution)/shard_map/ppermute | solution.py:48
  46.9 32.7 %copy-start.11 = (bf16[4,144,256]{2,1,0:T(8,128)(2,1)}, bf16[4,144,256]{2,1,0:T(8,128)(2,1)S(1)}, u32[]{:S(2)}) copy-start(bf16[4,144,256]{2,1,0:T(8,128)(2,1)S(1)} %pad_maximum_fusion.refs_0_) | copy-start | bytes 884740
  46.9 19.7 %collective-permute-start.9 = (bf16[4,144,256]{2,1,0:T(8,128)(2,1)S(1)}, bf16[4,144,256]{2,1,0:T(8,128)(2,1)S(1)}, u32[]{:S(2)}, u32[]{:S(2)}) collective-permute-start(bf16[4,144,256]{2,1,0:T(8,128)(2,1)S(1)} %pad_maximum_fusion.refs_0_), channel_id=1, source_target_pairs={{0,96},{8,104},{16,112},{24,120},{32,0},{40,8},{48,16},{56,24},{64... | collective-permute-start | bytes 884744 | tf_op jit(solution)/shard_map/ppermute | solution.py:48
  49.7 17.0 %collective-permute-start.8 = (bf16[4,144,256]{2,1,0:T(8,128)(2,1)S(1)}, bf16[4,144,256]{2,1,0:T(8,128)(2,1)S(1)}, u32[]{:S(2)}, u32[]{:S(2)}) collective-permute-start(bf16[4,144,256]{2,1,0:T(8,128)(2,1)S(1)} %pad_maximum_fusion.refs_0_), channel_id=1, source_target_pairs={{0,64},{8,72},{16,80},{24,88},{32,96},{40,104},{48,112},{56,120},{... | collective-permute-start | bytes 884744 | tf_op jit(solution)/shard_map/ppermute | solution.py:48
  50.5 29.0 %all-to-all-start = ((bf16[16,144,256]{2,1,0:T(8,128)(2,1)}), bf16[16,144,256]{2,1,0:T(8,128)(2,1)S(1)}, u32[]{:S(2)}, u32[]{:S(2)}) async-start(bf16[16,144,256]{2,1,0:T(8,128)(2,1)} %bitcast.8), calls=%async_computation | async-start | bytes 2359296 | tf_op jit(solution)/shard_map/all_to_all | solution.py:514
  56.8 106.8 %reduce-scatter.3.cloned.1.call-start = ((), (), s32[]{:S(2)}) async-start(), calls=%async_computation.6 | async-start | bytes 1310720 | tf_op jit(solution)/shard_map/reduce_scatter | solution.py:549
  56.9 21.6 %collective-permute-start.7 = (bf16[4,144,256]{2,1,0:T(8,128)(2,1)S(1)}, bf16[4,144,256]{2,1,0:T(8,128)(2,1)S(1)}, u32[]{:S(2)}, u32[]{:S(2)}) collective-permute-start(bf16[4,144,256]{2,1,0:T(8,128)(2,1)S(1)} %pad_maximum_fusion.refs_0_), channel_id=1, source_target_pairs={{0,32},{8,40},{16,48},{24,56},{32,64},{40,72},{48,80},{56,88},{64,... | collective-permute-start | bytes 884744 | tf_op jit(solution)/shard_map/ppermute | solution.py:48
  98.6 81.6 %reduce-scatter.5.cloned.1.call-start = ((), (), s32[]{:S(2)}) async-start(), calls=%async_computation.7 | async-start | bytes 5242880 | tf_op jit(solution)/shard_map/reduce_scatter | solution.py:552
  120.9 23.4 %copy-start.3 = (bf16[5120,128]{1,0:T(8,128)(2,1)S(1)}, bf16[5120,128]{1,0:T(8,128)(2,1)}, u32[]{:S(2)}) copy-start(bf16[5120,128]{1,0:T(8,128)(2,1)} %wk.1) | copy-start | bytes 3932164
  155.4 2.2 %collective-permute-start.10 = (bf16[4,16,5120]{2,1,0:T(8,128)(2,1)S(1)}, bf16[4,16,5120]{2,1,0:T(8,128)(2,1)S(1)}, u32[]{:S(2)}, u32[]{:S(2)}) collective-permute-start(bf16[4,16,5120]{2,1,0:T(8,128)(2,1)S(1)} %slice_bitcast_fusion), channel_id=1, source_target_pairs={{0,1},{1,0},{2,3},{3,2},{4,5},{5,4},{6,7},{7,6},{8,9},{9,8},{10,11... | collective-permute-start | bytes 1966088 | tf_op jit(solution)/shard_map/ppermute | solution.py:43
  159.4 7.7 %collective-permute-start.11 = (bf16[16,5120]{1,0:T(8,128)(2,1)}, bf16[16,5120]{1,0:T(8,128)(2,1)S(1)}, u32[]{:S(2)}, u32[]{:S(2)}) collective-permute-start(bf16[16,5120]{1,0:T(8,128)(2,1)} %get-tuple-element.60), channel_id=1, source_target_pairs={{0,2},{1,3},{2,4},{3,5},{4,6},{5,7},{6,0},{7,1},{8,10},{9,11},{10,... | collective-permute-start | bytes 491528 | tf_op jit(solution)/shard_map/ppermute | solution.py:43
  160.5 9.4 %collective-permute-start.13 = (bf16[16,5120]{1,0:T(8,128)(2,1)}, bf16[16,5120]{1,0:T(8,128)(2,1)S(1)}, u32[]{:S(2)}, u32[]{:S(2)}) collective-permute-start(bf16[16,5120]{1,0:T(8,128)(2,1)} %get-tuple-element.61), channel_id=1, source_target_pairs={{0,6},{1,7},{2,0},{3,1},{4,2},{5,3},{6,4},{7,5},{8,14},{9,15},{10,... | collective-permute-start | bytes 491528 | tf_op jit(solution)/shard_map/ppermute | solution.py:43
  162.6 9.0 %collective-permute-start.12 = (bf16[16,5120]{1,0:T(8,128)(2,1)}, bf16[16,5120]{1,0:T(8,128)(2,1)}, u32[]{:S(2)}, u32[]{:S(2)}) collective-permute-start(bf16[16,5120]{1,0:T(8,128)(2,1)} %get-tuple-element.62), channel_id=1, source_target_pairs={{0,4},{1,5},{2,6},{3,7},{4,0},{5,1},{6,2},{7,3},{8,12},{9,13},{10,... | collective-permute-start | bytes 491528 | tf_op jit(solution)/shard_map/ppermute | solution.py:43
  163.6 14.0 %all-to-all-start.1 = ((bf16[4,128,256]{2,1,0:T(8,128)(2,1)}), bf16[4,128,256]{2,1,0:T(8,128)(2,1)S(1)}, u32[]{:S(2)}, u32[]{:S(2)}) async-start(bf16[4,128,256]{2,1,0:T(8,128)(2,1)} %bitcast.43), calls=%async_computation.2 | async-start | bytes 524288 | tf_op jit(solution)/shard_map/all_to_all | solution.py:559
  (11 other events, 43.3 us)
Sparse Core Ops, SparseCore 0:
  10.2 66.5 all-gather.1
  98.7 22.1 reduce-scatter.2
  123.4 56.6 reduce-scatter.4
